TPU v7x, 32 devices: a whole 2x2x4 slice. The times are simulated.
32 devices in a mesh: grp: 2 (over x), gz: 16 (over z, y, core).
Axes of the slice: x: 2, y: 2, z: 4, core: 2. Of those that a mesh axis runs over, the one named last changes fastest.
Arguments:
- features: bfloat16 [12, 128, 32, 128], P(None, ('grp', 'gz')), parts along dimension 1, may hold values from -6 to 6
- w_first: bfloat16 [48, 324], replicated, may hold values from -0.5 to 0.5
- w_second: bfloat16 [96, 1296], replicated, may hold values from -0.25 to 0.25
- w_lift: bfloat16 [48, 96], replicated, may hold values from -0.875 to 0.875
- w_merge: bfloat16 [12, 1296], replicated, may hold values from -0.15625 to 0.15625
- w_affine: bfloat16 [3, 12], replicated, may hold values from -2.5 to 2.5
- tissue: int32 [32, 32], P(('grp', 'gz')), parts along dimension 0, may hold values from 0 to 31
- owners: int32 [32, 32], P(('grp', 'gz')), parts along dimension 0, may hold values from 0 to 15, as said below
Outputs:
- routed: bfloat16 [32, 16, 2, 1536], P(('grp', 'gz')), parts along dimension 0
There are 2 independent parts, one for each index of `grp`. A program takes and returns all parts, laid end to end along the dimension named above; an argument that names none is the same for every part. Nothing has to cross between parts.
Inputs may be any that keep to these rules, and one draw needn't show every extreme that they name: `owners`: A device sends at most 2 of its listed blocks to one owner; in every draw some owner receives exactly 2 from every device.
All inputs are finite; a program needn't handle non-finite values.
Results may differ from a plain program's by a relative error of at most 0.0054.
Values may be sent and summed in bfloat16 or wider, within the bound.
A program may use at most 128 MiB of HBM per device.

v0:
```python
import jax
import jax.numpy as jnp
from jax import lax
from jax.sharding import PartitionSpec as P

BY = 8
BX = 16
SEND_CAP = 2


def padded_2(cells, sides, width):
    for axis, dim in sides:
        count = lax.axis_size(axis)
        ends = count - 1
        head = lax.slice_in_dim(cells, 0, width, axis=dim)
        tail = lax.slice_in_dim(cells, cells.shape[dim] - width, cells.shape[dim], axis=dim)
        cells = jnp.concatenate(
            [
                lax.ppermute(tail, axis, [(i, (i + 1) % count) for i in range(ends)]),
                cells,
                lax.ppermute(head, axis, [((i + 1) % count, i) for i in range(ends)]),
            ],
            axis=dim,
        )
    return cells


def plane_terms(padded_plane, weight_slab):
    channels = padded_plane.shape[0]
    rows = padded_plane.shape[1] - 2
    columns = padded_plane.shape[2] - 2
    summed = jnp.zeros((weight_slab.shape[0], rows, columns), jnp.float32)
    for offset_y in range(3):
        stacked = jnp.concatenate(
            [
                padded_plane[:, offset_y : offset_y + rows, offset_x : offset_x + columns]
                for offset_x in range(3)
            ],
            axis=0,
        )
        weight_part = weight_slab[:, offset_y * 3 * channels : (offset_y + 1) * 3 * channels]
        summed = summed + jnp.einsum(
            "oi,iyx->oyx", weight_part, stacked, preferred_element_type=jnp.float32
        )
    return summed


def convolve(volume, weight, depth_pad):
    padded = jnp.pad(volume, ((0, 0), (depth_pad, depth_pad), (1, 1), (1, 1)))
    out_depth = padded.shape[1] - 2
    channels = volume.shape[0]

    def one_plane(plane_at):
        window_planes = lax.dynamic_slice_in_dim(padded, plane_at, 3, 1)
        summed = plane_terms(window_planes[:, 0], weight[:, 0 : 9 * channels])
        summed = summed + plane_terms(window_planes[:, 1], weight[:, 9 * channels : 18 * channels])
        summed = summed + plane_terms(window_planes[:, 2], weight[:, 18 * channels : 27 * channels])
        return summed

    planes = lax.map(one_plane, jnp.arange(out_depth, dtype=jnp.int32))
    return planes.transpose(1, 0, 2, 3)


def pad_plane(plane):
    return jnp.pad(plane, ((0, 0), (1, 1), (1, 1)))


def maxpool(volume):
    shape = volume.shape
    return volume.reshape(shape[0], shape[1] // 2, 2, shape[2] // 2, 2, shape[3] // 2, 2).max(
        axis=(2, 4, 6)
    )


def upsample(volume):
    shape = volume.shape
    spread = jnp.broadcast_to(
        volume[:, :, None, :, None, :, None], (shape[0], shape[1], 2, shape[2], 2, shape[3], 2)
    )
    return spread.reshape(shape[0], 2 * shape[1], 2 * shape[2], 2 * shape[3])


def on_device(features, w_first, w_second, w_lift, w_merge, w_affine, tissue, owners):
    depth = features.shape[1]
    widened = padded_2(features, (("gz", 1),), 1)
    first_map = jax.nn.relu(convolve(widened, w_first, 0)).astype(jnp.bfloat16)
    pooled_wide = padded_2(maxpool(first_map), (("gz", 1),), 1)
    second_map = jax.nn.relu(convolve(pooled_wide, w_second, 0)).astype(jnp.bfloat16)
    lifted = jnp.einsum("oc,czyx->ozyx", w_lift, second_map, preferred_element_type=jnp.float32)
    merged = (upsample(lifted) + first_map.astype(jnp.float32)).astype(jnp.bfloat16)
    inner = convolve(merged, w_merge, 1)
    channels = merged.shape[0]
    upward = plane_terms(pad_plane(merged[:, depth - 1]), w_merge[:, 0 : 9 * channels])[:, None]
    downward = plane_terms(pad_plane(merged[:, 0]), w_merge[:, 18 * channels : 27 * channels])[
        :, None
    ]
    edges = padded_2(
        jnp.concatenate([downward, upward], axis=1).astype(jnp.bfloat16), (("gz", 1),), 1
    ).astype(jnp.float32)
    lower_term = edges[:, :1]
    upper_term = edges[:, 3:]
    third_map = jnp.concatenate(
        [inner[:, :1] + lower_term, inner[:, 1 : depth - 1], inner[:, depth - 1 :] + upper_term],
        axis=1,
    )
    third_map = jax.nn.relu(third_map)
    affinity = jax.nn.sigmoid(
        jnp.einsum(
            "ac,czyx->azyx",
            w_affine.astype(jnp.float32),
            third_map,
            precision=lax.Precision.HIGHEST,
        )
    ).astype(jnp.bfloat16)
    shape = affinity.shape
    block_rows = shape[2] // BY
    block_cols = shape[3] // BX
    tiles = (
        affinity.reshape(shape[0], shape[1], block_rows, BY, block_cols, BX)
        .transpose(2, 4, 0, 1, 3, 5)
        .reshape(block_rows * block_cols, -1)
    )
    listed = tissue[0]
    owner_row = owners[0]
    count = listed.shape[0]
    devices = lax.axis_size("gz")
    slot_total = SEND_CAP * devices
    same_owner = owner_row[:, None] == owner_row[None, :]
    earlier = jnp.arange(count)[None, :] < jnp.arange(count)[:, None]
    ranks = jnp.sum(same_owner & earlier, axis=1)
    slot_index = owner_row * SEND_CAP + ranks
    slot_pick = (slot_index[:, None] == jnp.arange(slot_total, dtype=jnp.int32)[None, :]).astype(
        jnp.bfloat16
    )
    block_pick = (listed[:, None] == jnp.arange(tiles.shape[0], dtype=jnp.int32)[None, :]).astype(
        jnp.bfloat16
    )
    select = jnp.dot(slot_pick.T, block_pick, preferred_element_type=jnp.float32).astype(
        jnp.bfloat16
    )
    outgoing = jnp.dot(select, tiles, preferred_element_type=jnp.float32).astype(jnp.bfloat16)
    outgoing = outgoing.reshape(devices, SEND_CAP, tiles.shape[1])
    received = lax.all_to_all(outgoing, "gz", split_axis=0, concat_axis=0, tiled=True)
    return received[None]


def solution(mesh):
    placed = (
        P(None, ("grp", "gz"), None, None),
        P(),
        P(),
        P(),
        P(),
        P(),
        P(("grp", "gz"), None),
        P(("grp", "gz"), None),
    )
    return jax.shard_map(
        on_device,
        mesh=mesh,
        in_specs=placed,
        out_specs=P(("grp", "gz"), None, None, None),
        check_vma=False,
    )
```

profile of v0, /device:TPU:0, one launch (start us, length us, event | category | flops | bytes accessed | tf_op | source)
XLA Modules:
  0.0 166.6 jit_solution(14068969063575705335)
XLA Ops:
  0.0 1.3 copy.24
  1.3 2.4 %collective-permute-start = (bf16[12,1,32,128]{3,0,2,1:T(8,128)(2,1)S(1)}, bf16[12,1,32,128]{3,0,2,1:T(8,128)(2,1)S(1)}, u32[]{:S(2)}, u32[]{:S(2)}) collective-permute-start(bf16[12,1,32,128]{3,0,2,1:T(8,128)(2,1)S(1)} %get-tuple-element.272), channel_id=1, source_target_pairs={{0,1},{1,2},{2,3},{3,4},{4,5},{5,6},{6,7},{7,8},{8,9},{9,10},{10,1... | collective-permute-start | bytes 294920 | tf_op jit(solution)/shard_map/ppermute | solution.py:19
  3.7 1.3 collective-permute-start.1
  5.0 0.9 copy.27
  5.9 0.9 convert_reduce_fusion
  6.8 2.4 %collective-permute-done.1 = bf16[12,1,32,128]{3,0,2,1:T(8,128)(2,1)} collective-permute-done((bf16[12,1,32,128]{3,0,2,1:T(8,128)(2,1)S(1)}, bf16[12,1,32,128]{3,0,2,1:T(8,128)(2,1)}, u32[]{:S(2)}, u32[]{:S(2)}) %collective-permute-start.1) | collective-permute-done | bytes 98336 | tf_op jit(solution)/shard_map/ppermute | solution.py:21
  9.2 2.1 %select_maximum_fusion = bf16[12,6,34,130]{3,0,2,1:T(8,128)(2,1)S(1)} fusion(bf16[12,1,32,128]{3,0,2,1:T(8,128)(2,1)} %collective-permute-done.1, bf16[12,4,32,128]{3,0,2,1:T(8,128)(2,1)} %copy-done.3, bf16[12,1,32,128]{3,0,2,1:T(8,128)(2,1)S(1)} %collective-permute-done), kind=kLoop, calls=%fused_computation.303 | loop fusion | flops 6046560 | bytes 1226304 | tf_op jit(solution)/shard_map/concatenate | solution.py:17
  11.3 26.7 %while.33 = (s32[]{:T(128)}, bf16[4,48,32,128]{3,1,2,0:T(8,128)(2,1)S(1)}, s32[4]{0:T(128)S(1)}, bf16[12,6,34,130]{3,0,2,1:T(8,128)(2,1)S(1)}, bf16[48,324]{0,1:T(8,128)(2,1)S(1)}) while((s32[]{:T(128)}, bf16[4,48,32,128]{3,1,2,0:T(8,128)(2,1)S(1)}, s32[4]{0:T(128)S(1)}, bf16[12,6,34,130]{3,0,2,1:T(8,128)(2,1)S(1)}, ...), condition=%wide.region_2.3_spmd.clone, body=%wide.region_1.2_spmd.sunk.clone | while | flops 136937472 | bytes 22945500 | solution.py:60
  11.3 0.7 dynamic_slice.26
  15.4 0.6 fusion.573
  18.0 0.7 dynamic_slice.26
  22.1 0.6 fusion.573
  24.7 0.7 dynamic_slice.26
  28.7 0.6 fusion.573
  31.3 0.7 dynamic_slice.26
  35.4 0.6 fusion.573
  38.3 3.1 %copy.28 = bf16[48,4,32,128]{0,3,2,1:T(8,128)(2,1)} copy(bf16[48,4,32,128]{3,0,2,1:T(8,128)(2,1)S(1)} %fusion.278) | data formatting | bytes 3145728 | tf_op jit(solution)/shard_map/convert_element_type | solution.py:86
  41.4 8.4 %reduce_max.9 = bf16[48,2,16,64]{0,3,2,1:T(8,128)(2,1)S(1)} reduce(bf16[48,2,2,16,2,64,2]{0,6,5,4,3,2,1:T(2,128)(2,1)} %bitcast.293, bf16[]{:T(256)} %constant.41.clone.1), dimensions={2,4,6}, to_apply=%region_3.4 | reduce | flops 688128 | bytes 1769474 | tf_op jit(solution)/shard_map/reduce_max | solution.py:70
  49.9 5.4 %collective-permute-start.2 = (bf16[48,1,16,64]{0,3,2,1:T(8,128)(2,1)S(1)}, bf16[48,1,16,64]{0,3,2,1:T(8,128)(2,1)S(1)}, u32[]{:S(2)}, u32[]{:S(2)}) collective-permute-start(bf16[48,1,16,64]{0,3,2,1:T(8,128)(2,1)S(1)} %get-tuple-element.270), channel_id=1, source_target_pairs={{0,1},{1,2},{2,3},{3,4},{4,5},{5,6},{6,7},{7,8},{8,9},{9,10},{10,1... | collective-permute-start | bytes 294920 | tf_op jit(solution)/shard_map/ppermute | solution.py:19
  55.3 1.5 collective-permute-start.3
  57.1 1.7 collective-permute-done.3
  59.2 17.8 %while.34 = (s32[]{:T(128)}, bf16[2,96,16,64]{1,3,2,0:T(8,128)(2,1)S(1)}, s32[2]{0:T(128)S(1)}, bf16[48,4,18,66]{0,3,2,1:T(8,128)(2,1)S(1)}, bf16[96,1296]{0,1:T(8,128)(2,1)S(1)}) while((s32[]{:T(128)}, bf16[2,96,16,64]{1,3,2,0:T(8,128)(2,1)S(1)}, s32[2]{0:T(128)S(1)}, bf16[48,4,18,66]{0,3,2,1:T(8,128)(2,1)S(1)}, ...), condition=%wide.region_5.6_spmd.clone, body=%wide.region_4.5_spmd.sunk.clone | while | flops 263553024 | bytes 21135772 | solution.py:60
  59.2 0.7 dynamic_slice.27
  64.0 0.9 fusion.598
  65.5 0.5 convolution_add_fusion.34
  66.0 0.5 fusion.600
  67.5 0.6 fusion.602
  68.1 0.7 dynamic_slice.27
  73.0 0.9 fusion.598
  74.4 0.5 convolution_add_fusion.34
  74.9 0.5 fusion.600
  76.4 0.6 fusion.602
  77.1 0.6 convolution_bitcast_fusion
  78.0 7.5 %broadcast_in_dim.46 = f32[48,2,2,16,2,64,2]{0,6,5,4,3,2,1:T(2,128)} broadcast(f32[48,2,16,64]{0,3,2,1:T(8,128)S(1)} %copy.30), dimensions={0,1,3,5} | broadcast | bytes 3538944 | tf_op jit(solution)/shard_map/broadcast_in_dim | solution.py:77
  85.5 5.1 %copy.31 = f32[48,4,32,128]{3,0,2,1:T(8,128)S(1)} copy(f32[48,4,32,128]{0,3,2,1:T(8,128)} %bitcast.292) | data formatting | bytes 6291456 | tf_op jit(solution)/shard_map/reshape | solution.py:80
  90.7 1.9 %add_convert_fusion = bf16[48,4,32,128]{3,0,2,1:T(8,128)(2,1)S(1)} fusion(f32[48,4,32,128]{3,0,2,1:T(8,128)S(1)} %copy.31, bf16[4,48,32,128]{3,1,2,0:T(8,128)(2,1)} %copy-done.2), kind=kLoop, calls=%fused_computation.281 | loop fusion | flops 4718592 | bytes 6291456 | tf_op jit(solution)/shard_map/convert_element_type | solution.py:90
  92.6 0.7 pad_slice_fusion.10
  94.3 7.2 %collective-permute-start.4 = (bf16[12,1,32,128]{3,0,2,1:T(8,128)(2,1)S(1)}, bf16[12,1,32,128]{3,0,2,1:T(8,128)(2,1)S(1)}, u32[]{:S(2)}, u32[]{:S(2)}) collective-permute-start(bf16[12,1,32,128]{3,0,2,1:T(8,128)(2,1)S(1)} %fusion.344), channel_id=1, source_target_pairs={{0,1},{1,2},{2,3},{3,4},{4,5},{5,6},{6,7},{7,8},{8,9},{9,10},{10,1... | collective-permute-start | bytes 294920 | tf_op jit(solution)/shard_map/ppermute | solution.py:19
  101.5 0.7 pad_slice_fusion.2
  103.2 1.4 collective-permute-start.5
  104.6 3.5 %pad.21 = bf16[48,6,34,130]{3,0,2,1:T(8,128)(2,1)} pad(bf16[48,4,32,128]{3,0,2,1:T(8,128)(2,1)S(1)} %add_convert_fusion, bf16[]{:T(256)} %constant.39.clone.1), padding=0_0x1_1x1_1x1_1 | pad | bytes 4118786 | tf_op jit(solution)/shard_map/jit(_pad)/pad | solution.py:49
  108.1 39.1 %while.35 = (s32[]{:T(128)}, f32[4,12,32,128]{3,1,2,0:T(8,128)S(1)}, s32[4]{0:T(128)S(1)}, bf16[48,6,34,130]{3,0,2,1:T(8,128)(2,1)}, bf16[12,1296]{1,0:T(8,128)(2,1)S(1)}) while((s32[]{:T(128)}, f32[4,12,32,128]{3,1,2,0:T(8,128)S(1)}, s32[4]{0:T(128)S(1)}, bf16[48,6,34,130]{3,0,2,1:T(8,128)(2,1)}, ...), condition=%wide.region_7.8_spmd.clone, body=%wide.region_6.7_spmd.sunk.clone | while | flops 159645696 | bytes 38402460 | solution.py:60
  108.1 0.6 dynamic_slice.28
  110.7 1.8 %dynamic-slice_bitcast_fusion.17 = (bf16[48,34,130]{2,0,1:T(8,128)(2,1)S(1)}, bf16[48,34,130]{2,0,1:T(8,128)(2,1)S(1)}, bf16[48,34,130]{2,0,1:T(8,128)(2,1)S(1)}) fusion(bf16[48,6,34,130]{3,0,2,1:T(8,128)(2,1)} %get-tuple-element.744, s32[]{:T(128)S(6)} %add.376, s32[]{:T(128)S(6)} %add.377, s32[]{:T(128)S(6)} %select_n.17), kind=kLoop, calls=%fused_computation.240.clone.1.clone | loop fusion | bytes 2545932 | tf_op jit(solution)/shard_map/while/body/eval_jaxpr/squeeze | solution.py:57
  112.5 0.8 fusion.621
  114.2 1.8 %fusion.625 = (bf16[48,32,128]{2,0,1:T(8,128)(2,1)S(1)}, bf16[48,32,128]{2,0,1:T(8,128)(2,1)S(1)}, bf16[48,32,128]{2,0,1:T(8,128)(2,1)S(1)}, bf16[48,32,128]{2,0...) fusion(bf16[48,34,130]{2,0,1:T(8,128)(2,1)S(1)} %get-tuple-elem, ...), kind=kLoop, calls=%fused_computation.419.clone.1.clone | loop fusion | bytes 14155776 | tf_op jit(solution)/shard_map/while/body/eval_jaxpr/slice | solution.py:36
  117.9 0.6 dynamic_slice.28
  120.4 1.8 %dynamic-slice_bitcast_fusion.17 = (bf16[48,34,130]{2,0,1:T(8,128)(2,1)S(1)}, bf16[48,34,130]{2,0,1:T(8,128)(2,1)S(1)}, bf16[48,34,130]{2,0,1:T(8,128)(2,1)S(1)}) fusion(bf16[48,6,34,130]{3,0,2,1:T(8,128)(2,1)} %get-tuple-element.744, s32[]{:T(128)S(6)} %add.376, s32[]{:T(128)S(6)} %add.377, s32[]{:T(128)S(6)} %select_n.17), kind=kLoop, calls=%fused_computation.240.clone.1.clone | loop fusion | bytes 2545932 | tf_op jit(solution)/shard_map/while/body/eval_jaxpr/squeeze | solution.py:57
  122.3 0.8 fusion.621
  124.0 1.8 %fusion.625 = (bf16[48,32,128]{2,0,1:T(8,128)(2,1)S(1)}, bf16[48,32,128]{2,0,1:T(8,128)(2,1)S(1)}, bf16[48,32,128]{2,0,1:T(8,128)(2,1)S(1)}, bf16[48,32,128]{2,0...) fusion(bf16[48,34,130]{2,0,1:T(8,128)(2,1)S(1)} %get-tuple-elem, ...), kind=kLoop, calls=%fused_computation.419.clone.1.clone | loop fusion | bytes 14155776 | tf_op jit(solution)/shard_map/while/body/eval_jaxpr/slice | solution.py:36
  127.7 0.6 dynamic_slice.28
  130.2 1.8 %dynamic-slice_bitcast_fusion.17 = (bf16[48,34,130]{2,0,1:T(8,128)(2,1)S(1)}, bf16[48,34,130]{2,0,1:T(8,128)(2,1)S(1)}, bf16[48,34,130]{2,0,1:T(8,128)(2,1)S(1)}) fusion(bf16[48,6,34,130]{3,0,2,1:T(8,128)(2,1)} %get-tuple-element.744, s32[]{:T(128)S(6)} %add.376, s32[]{:T(128)S(6)} %add.377, s32[]{:T(128)S(6)} %select_n.17), kind=kLoop, calls=%fused_computation.240.clone.1.clone | loop fusion | bytes 2545932 | tf_op jit(solution)/shard_map/while/body/eval_jaxpr/squeeze | solution.py:57
  132.1 0.8 fusion.621
  133.8 1.8 %fusion.625 = (bf16[48,32,128]{2,0,1:T(8,128)(2,1)S(1)}, bf16[48,32,128]{2,0,1:T(8,128)(2,1)S(1)}, bf16[48,32,128]{2,0,1:T(8,128)(2,1)S(1)}, bf16[48,32,128]{2,0...) fusion(bf16[48,34,130]{2,0,1:T(8,128)(2,1)S(1)} %get-tuple-elem, ...), kind=kLoop, calls=%fused_computation.419.clone.1.clone | loop fusion | bytes 14155776 | tf_op jit(solution)/shard_map/while/body/eval_jaxpr/slice | solution.py:36
  137.5 0.6 dynamic_slice.28
  140.0 1.8 %dynamic-slice_bitcast_fusion.17 = (bf16[48,34,130]{2,0,1:T(8,128)(2,1)S(1)}, bf16[48,34,130]{2,0,1:T(8,128)(2,1)S(1)}, bf16[48,34,130]{2,0,1:T(8,128)(2,1)S(1)}) fusion(bf16[48,6,34,130]{3,0,2,1:T(8,128)(2,1)} %get-tuple-element.744, s32[]{:T(128)S(6)} %add.376, s32[]{:T(128)S(6)} %add.377, s32[]{:T(128)S(6)} %select_n.17), kind=kLoop, calls=%fused_computation.240.clone.1.clone | loop fusion | bytes 2545932 | tf_op jit(solution)/shard_map/while/body/eval_jaxpr/squeeze | solution.py:57
  141.9 0.8 fusion.621
  143.6 1.8 %fusion.625 = (bf16[48,32,128]{2,0,1:T(8,128)(2,1)S(1)}, bf16[48,32,128]{2,0,1:T(8,128)(2,1)S(1)}, bf16[48,32,128]{2,0,1:T(8,128)(2,1)S(1)}, bf16[48,32,128]{2,0...) fusion(bf16[48,34,130]{2,0,1:T(8,128)(2,1)S(1)} %get-tuple-elem, ...), kind=kLoop, calls=%fused_computation.419.clone.1.clone | loop fusion | bytes 14155776 | tf_op jit(solution)/shard_map/while/body/eval_jaxpr/slice | solution.py:36
  147.5 0.5 copy-done.8
  148.0 0.7 fusion.340
  148.7 0.5 reshape.28
  149.4 1.2 reshape.29
  151.1 14.8 %all_to_all.5 = bf16[16,2,1536]{2,1,0:T(2,128)(2,1)S(1)} all-to-all(bf16[16,2,1536]{2,1,0:T(2,128)(2,1)S(1)} %reshape.30), channel_id=1, replica_groups=mesh['grp'=2,'gz'=16] {'gz'}, dimensions={0} | all-to-all | bytes 196608 | tf_op jit(solution)/shard_map/all_to_all | solution.py:143
  166.0 0.6 copy.60
  (145 shorter events, 35.6 us)
Async XLA Ops:
  0.0 77.1 %copy-start = (bf16[48,96]{1,0:T(8,128)(2,1)S(1)}, bf16[48,96]{1,0:T(8,128)(2,1)}, u32[]{:S(2)}) copy-start(bf16[48,96]{1,0:T(8,128)(2,1)} %param.17) | copy-start | bytes 27652
  1.3 2.4 %copy-start.3 = (bf16[12,4,32,128]{3,0,2,1:T(8,128)(2,1)}, bf16[12,4,32,128]{3,0,2,1:T(8,128)(2,1)S(1)}, u32[]{:S(2)}) copy-start(bf16[12,4,32,128]{3,0,2,1:T(8,128)(2,1)S(1)} %copy.24) | copy-start | bytes 1179652
  1.3 5.5 %collective-permute-start = (bf16[12,1,32,128]{3,0,2,1:T(8,128)(2,1)S(1)}, bf16[12,1,32,128]{3,0,2,1:T(8,128)(2,1)S(1)}, u32[]{:S(2)}, u32[]{:S(2)}) collective-permute-start(bf16[12,1,32,128]{3,0,2,1:T(8,128)(2,1)S(1)} %get-tuple-element.272), channel_id=1, source_target_pairs={{0,1},{1,2},{2,3},{3,4},{4,5},{5,6},{6,7},{7,8},{8,9},{9,10},{10,1... | collective-permute-start | bytes 294920 | tf_op jit(solution)/shard_map/ppermute | solution.py:19
  3.7 5.5 %collective-permute-start.1 = (bf16[12,1,32,128]{3,0,2,1:T(8,128)(2,1)S(1)}, bf16[12,1,32,128]{3,0,2,1:T(8,128)(2,1)}, u32[]{:S(2)}, u32[]{:S(2)}) collective-permute-start(bf16[12,1,32,128]{3,0,2,1:T(8,128)(2,1)S(1)} %get-tuple-element.273), channel_id=1, source_target_pairs={{1,0},{2,1},{3,2},{4,3},{5,4},{6,5},{7,6},{8,7},{9,8},{10,9},{11,1... | collective-permute-start | bytes 294920 | tf_op jit(solution)/shard_map/ppermute | solution.py:21
  38.0 3.5 %copy-start.2 = (bf16[4,48,32,128]{3,1,2,0:T(8,128)(2,1)}, bf16[4,48,32,128]{3,1,2,0:T(8,128)(2,1)S(1)}, u32[]{:S(2)}) copy-start(bf16[4,48,32,128]{3,1,2,0:T(8,128)(2,1)S(1)} %get-tuple-element.86) | copy-start | bytes 4718596
  41.4 15.3 %copy-start.9 = (s32[1,32]{1,0:T(1,128)S(1)}, s32[1,32]{1,0:T(1,128)}, u32[]{:S(2)}) copy-start(s32[1,32]{1,0:T(1,128)} %param.21) | copy-start | bytes 388
  41.4 15.4 %copy-start.5 = (bf16[96,1296]{1,0:T(8,128)(2,1)S(1)}, bf16[96,1296]{1,0:T(8,128)(2,1)}, u32[]{:S(2)}) copy-start(bf16[96,1296]{1,0:T(8,128)(2,1)} %param.16) | copy-start | bytes 746500
  49.9 7.2 %collective-permute-start.2 = (bf16[48,1,16,64]{0,3,2,1:T(8,128)(2,1)S(1)}, bf16[48,1,16,64]{0,3,2,1:T(8,128)(2,1)S(1)}, u32[]{:S(2)}, u32[]{:S(2)}) collective-permute-start(bf16[48,1,16,64]{0,3,2,1:T(8,128)(2,1)S(1)} %get-tuple-element.270), channel_id=1, source_target_pairs={{0,1},{1,2},{2,3},{3,4},{4,5},{5,6},{6,7},{7,8},{8,9},{9,10},{10,1... | collective-permute-start | bytes 294920 | tf_op jit(solution)/shard_map/ppermute | solution.py:19
  55.3 3.4 %collective-permute-start.3 = (bf16[48,1,16,64]{0,3,2,1:T(8,128)(2,1)S(1)}, bf16[48,1,16,64]{0,3,2,1:T(8,128)(2,1)S(1)}, u32[]{:S(2)}, u32[]{:S(2)}) collective-permute-start(bf16[48,1,16,64]{0,3,2,1:T(8,128)(2,1)S(1)} %get-tuple-element.271), channel_id=1, source_target_pairs={{1,0},{2,1},{3,2},{4,3},{5,4},{6,5},{7,6},{8,7},{9,8},{10,9},{11,1... | collective-permute-start | bytes 294920 | tf_op jit(solution)/shard_map/ppermute | solution.py:21
  92.6 0.8 copy-start.7
  94.3 53.0 %collective-permute-start.4 = (bf16[12,1,32,128]{3,0,2,1:T(8,128)(2,1)S(1)}, bf16[12,1,32,128]{3,0,2,1:T(8,128)(2,1)S(1)}, u32[]{:S(2)}, u32[]{:S(2)}) collective-permute-start(bf16[12,1,32,128]{3,0,2,1:T(8,128)(2,1)S(1)} %fusion.344), channel_id=1, source_target_pairs={{0,1},{1,2},{2,3},{3,4},{4,5},{5,6},{6,7},{7,8},{8,9},{9,10},{10,1... | collective-permute-start | bytes 294920 | tf_op jit(solution)/shard_map/ppermute | solution.py:19
  103.2 5.0 %copy-start.4 = (f32[4,12,32,128]{3,1,2,0:T(8,128)S(1)}, f32[4,12,32,128]{3,1,2,0:T(8,128)}, u32[]{:S(2)}) copy-start(f32[4,12,32,128]{3,1,2,0:T(8,128)} %custom-call) | copy-start | bytes 2359300
  103.2 44.2 %collective-permute-start.5 = (bf16[12,1,32,128]{3,0,2,1:T(8,128)(2,1)S(1)}, bf16[12,1,32,128]{3,0,2,1:T(8,128)(2,1)S(1)}, u32[]{:S(2)}, u32[]{:S(2)}) collective-permute-start(bf16[12,1,32,128]{3,0,2,1:T(8,128)(2,1)S(1)} %fusion.341), channel_id=1, source_target_pairs={{1,0},{2,1},{3,2},{4,3},{5,4},{6,5},{7,6},{8,7},{9,8},{10,9},{11,1... | collective-permute-start | bytes 294920 | tf_op jit(solution)/shard_map/ppermute | solution.py:21
  147.3 0.7 copy-start.8
  148.7 1.9 %copy-start.6 = (s32[1,32]{1,0:T(1,128)S(1)}, s32[1,32]{1,0:T(1,128)}, u32[]{:S(2)}) copy-start(s32[1,32]{1,0:T(1,128)} %param.20) | copy-start | bytes 388
  148.7 17.9 %copy-start.1 = (bf16[48,96]{1,0:T(8,128)(2,1)S(1)}, bf16[48,96]{1,0:T(8,128)(2,1)}, u32[]{:S(2)}) copy-start(bf16[48,96]{1,0:T(8,128)(2,1)} %param.17) | copy-start | bytes 27652
where the time goes:
time: 168 us; the launch traced here: 167 us
  local copies, waits for them, and re-layouts  57.6 us (34%)
  matrix products  35.7 us (21%)
  loops' own time  20.7 us (12%)
  starting transfers between devices  19.2 us (11%)
  blocking collectives  14.8 us (9%)
  other arithmetic  14.1 us (8%)
  waiting for transfers between devices  4.06 us (2%)
    dot_general x96, matrix products, plane_terms(): jnp.einsum('oi,iyx->oyx', weight_part, stacked, preferred_element_type=jn...  34 us
    another operation x3, loops' own time, convolve(): planes = lax.map(one_plane, jnp.arange(out_depth, dtype=jnp.int32))  20.7 us
    slice x22, local copies, waits for them, and re-layouts, plane_terms(): padded_plane[:, offset_y:offset_y + rows, offset_x:offset_x + columns]  18.1 us
    ppermute x3, starting transfers between devices, padded_2(): lax.ppermute(tail, axis, [(i, (i + 1) % count) for i in range(ends)])  15 us
    all_to_all x1, blocking collectives, on_device(): lax.all_to_all(outgoing, 'gz', split_axis=0, concat_axis=0, tiled=True)  14.8 us
    reduce_max x1, other arithmetic, maxpool(): volume.reshape(shape[0], shape[1] // 2, 2, shape[2] // 2, 2, shape[3] //...  8.37 us
    squeeze x10, local copies, waits for them, and re-layouts, one_plane(): window_planes[:, 2]  7.71 us
    broadcast_in_dim x1, local copies, waits for them, and re-layouts, upsample(): jnp.broadcast_to(volume[:, :, None, :, None, :, None], (shape[0], shape[1...  7.5 us
  transfers between devices with their start and end apart: 6, of which 2 were waited for; matrix products, arithmetic and copies ran while one was open for 23% of the time, Pallas kernels for 0%

commit v1 on v0

v1 whole, which is shorter than its diff:
```python
import functools

import jax
import jax.numpy as jnp
from jax import lax
from jax.experimental import pallas as pl
from jax.experimental.pallas import tpu as pltpu
from jax.sharding import PartitionSpec as P

BY = 8
BX = 16
SEND_CAP = 2
LANES = 128
ROWS = 16
F32 = jnp.float32
BF16 = jnp.bfloat16


def lane_shift(tile, step, lane):
    rolled = pltpu.roll(tile, step % LANES, axis=1)
    keep = lane >= step if step > 0 else lane < LANES + step
    return jnp.where(keep, rolled, 0.0)


def kernel(
    n, ny,
    f_ref, w1_ref, w2_ref, wl_ref, w3_ref, wa_ref, tissue_ref, owners_ref,
    out_ref,
    fhalo, xpad, fmap, pool, mpad, terms, edge, ehalo, tiles, outgoing,
    fsend, frecv, psend, precv, esend, erecv, asend, arecv,
):
    me = lax.axis_index("gz")
    has_left = me > 0
    has_right = me < n - 1
    left = me - 1
    right = me + 1
    cells = ny * LANES
    hy = ny // 2
    hcells = hy * LANES

    barrier = pltpu.get_barrier_semaphore()

    def greet(step, _):
        pl.semaphore_signal(
            barrier, inc=1, device_id={"gz": lax.rem(me + step, n)},
            device_id_type=pl.DeviceIdType.MESH,
        )
        return 0

    lax.fori_loop(1, n, greet, 0)

    def lanes_of(rows):
        return lax.broadcasted_iota(jnp.int32, (rows, LANES), 1)

    xpad[:, 0:LANES] = jnp.zeros((240, LANES), BF16)
    xpad[:, cells + LANES : cells + 2 * LANES] = jnp.zeros((240, LANES), BF16)
    pool[:, 0:LANES] = jnp.zeros((576, LANES), BF16)
    pool[:, hcells + LANES : hcells + 2 * LANES] = jnp.zeros((576, LANES), BF16)
    mpad[:, 0:LANES] = jnp.zeros((192, LANES), BF16)
    mpad[:, cells + LANES : cells + 2 * LANES] = jnp.zeros((192, LANES), BF16)

    def remote(src, dst, send, recv, target):
        return pltpu.make_async_remote_copy(
            src_ref=src, dst_ref=dst, send_sem=send, recv_sem=recv,
            device_id={"gz": target}, device_id_type=pl.DeviceIdType.MESH,
        )

    def exchange(to_left, at_right, to_right, at_left, send, recv):
        go_left = remote(to_left, at_right, send.at[0], recv.at[0], left)
        go_right = remote(to_right, at_left, send.at[1], recv.at[1], right)

        def start():
            @pl.when(has_left)
            def _():
                go_left.start()

            @pl.when(has_right)
            def _():
                go_right.start()

        def finish():
            @pl.when(has_right)
            def _():
                go_left.wait_recv()

            @pl.when(has_left)
            def _():
                go_right.wait_recv()

            @pl.when(has_left)
            def _():
                go_left.wait_send()

            @pl.when(has_right)
            def _():
                go_right.wait_send()

            @pl.when(jnp.logical_not(has_right))
            def _():
                at_right[...] = jnp.zeros(at_right.shape, at_right.dtype)

            @pl.when(jnp.logical_not(has_left))
            def _():
                at_left[...] = jnp.zeros(at_left.shape, at_left.dtype)

        return start, finish

    pl.semaphore_wait(barrier, n - 1)

    start, finish = exchange(
        f_ref.at[0:16], fhalo.at[16:32], f_ref.at[32:48], fhalo.at[0:16], fsend, frecv
    )
    start()
    finish()

    def shift_features(y, _):
        at = pl.ds(pl.multiple_of(y * LANES, LANES), LANES)
        to = pl.ds(pl.multiple_of((y + 1) * LANES, LANES), LANES)
        lane = lanes_of(80)
        v = jnp.concatenate([fhalo[0:16, at], f_ref[:, at], fhalo[16:32, at]], axis=0)
        vf = v.astype(F32)
        xpad[0:80, to] = lane_shift(vf, 1, lane).astype(BF16)
        xpad[80:160, to] = v
        xpad[160:240, to] = lane_shift(vf, -1, lane).astype(BF16)
        return 0

    lax.fori_loop(0, ny, shift_features, 0, unroll=2)

    def shift_pool(row0, rows, v, to):
        lane = lanes_of(rows)
        pool[row0 : row0 + rows, to] = lane_shift(v, 2, lane).astype(BF16)
        pool[384 + row0 : 384 + row0 + rows, to] = lane_shift(v, -2, lane).astype(BF16)

    def first_conv(i, _):
        base = pl.multiple_of(i * 2 * LANES, 2 * LANES)
        patch = jnp.concatenate(
            [
                xpad[:, pl.ds(pl.multiple_of(base + b * LANES, LANES), 2 * LANES)]
                for b in range(3)
            ],
            axis=0,
        )
        acc = jnp.maximum(jnp.dot(w1_ref[...], patch, preferred_element_type=F32), 0.0)
        fmap[:, pl.ds(base, 2 * LANES)] = acc.astype(BF16)
        deep = jnp.concatenate(
            [jnp.maximum(acc[0:48], acc[48:96]), jnp.maximum(acc[96:144], acc[144:192])], axis=0
        )
        wide = jnp.maximum(deep[:, 0:LANES], deep[:, LANES : 2 * LANES])
        even = lax.rem(lanes_of(96), 2) == 0
        other = jnp.where(
            even, pltpu.roll(wide, LANES - 1, axis=1), pltpu.roll(wide, 1, axis=1)
        )
        both = jnp.maximum(wide, other)
        to = pl.ds(pl.multiple_of((i + 1) * LANES, LANES), LANES)
        pool[240:336, to] = both.astype(BF16)
        shift_pool(48, 96, both, to)
        return 0

    lax.fori_loop(0, hy, first_conv, 0, unroll=2)

    inner = pl.ds(LANES, hcells)
    start, finish = exchange(
        pool.at[240:288, inner], pool.at[336:384, inner],
        pool.at[288:336, inner], pool.at[192:240, inner], psend, precv,
    )
    start()
    finish()

    def shift_halo(y, _):
        to = pl.ds(pl.multiple_of((y + 1) * LANES, LANES), LANES)
        shift_pool(0, 48, pool[192:240, to].astype(F32), to)
        shift_pool(144, 48, pool[336:384, to].astype(F32), to)
        return 0

    lax.fori_loop(0, hy, shift_halo, 0, unroll=2)

    def second_conv(i, _):
        base = pl.multiple_of(i * 2 * LANES, 2 * LANES)
        patch = jnp.concatenate(
            [
                pool[:, pl.ds(pl.multiple_of(base + b * LANES, LANES), 2 * LANES)]
                for b in range(3)
            ],
            axis=0,
        )
        acc = jnp.dot(w2_ref[...], patch, preferred_element_type=F32)
        second = jnp.maximum(acc, 0.0).astype(BF16)
        for half in range(2):
            lifted = jnp.dot(
                wl_ref[...], second[96 * half : 96 * half + 96], preferred_element_type=F32
            )
            for row in range(4):
                part = lifted[:, (row // 2) * LANES : (row // 2 + 1) * LANES]
                for deep in range(2):
                    plane = 48 * (2 * half + deep)
                    own = fmap[
                        plane : plane + 48,
                        pl.ds(pl.multiple_of(i * 4 * LANES + row * LANES, LANES), LANES),
                    ]
                    mpad[
                        plane : plane + 48,
                        pl.ds(pl.multiple_of(i * 4 * LANES + (row + 1) * LANES, LANES), LANES),
                    ] = (part + own.astype(F32)).astype(BF16)
        return 0

    lax.fori_loop(0, hy // 2, second_conv, 0)

    def third_conv(i, _):
        base = pl.multiple_of(i * 2 * LANES, 2 * LANES)
        patch = jnp.concatenate(
            [
                mpad[:, pl.ds(pl.multiple_of(base + b * LANES, LANES), 2 * LANES)]
                for b in range(3)
            ],
            axis=0,
        )
        acc = jnp.dot(w3_ref[...], patch, preferred_element_type=F32)
        lane = lanes_of(72)
        for row in range(2):
            at = slice(row * LANES, (row + 1) * LANES)
            total = (
                acc[72:144, at]
                + lane_shift(acc[0:72, at], 1, lane)
                + lane_shift(acc[144:216, at], -1, lane)
            )
            to = pl.ds(pl.multiple_of(base + row * LANES, LANES), LANES)
            terms[:, to] = total
            edge[0:16, to] = total[0:16].astype(BF16)
            edge[16:32, to] = total[56:72].astype(BF16)
        return 0

    lax.fori_loop(0, hy, third_conv, 0, unroll=2)

    start, finish = exchange(
        edge.at[0:16], ehalo.at[16:32], edge.at[16:32], ehalo.at[0:16], esend, erecv
    )
    start()
    finish()

    spread_row = lax.broadcasted_iota(jnp.int32, (BY * LANES, LANES), 0)
    spread_col = lax.broadcasted_iota(jnp.int32, (BY * LANES, LANES), 1)
    spread = jnp.where(
        spread_col == (spread_row // LANES) * BX + lax.rem(spread_row, BX), 1.0, 0.0
    ).astype(BF16)
    nbx = LANES // BX
    block_mask = (
        lax.broadcasted_iota(jnp.int32, (nbx * ROWS, LANES), 0) // ROWS
        == lax.broadcasted_iota(jnp.int32, (nbx * ROWS, LANES), 1) // BX
    )

    def head(by, _):
        parts = []
        for pair in range(BY // 2):
            at = pl.ds(pl.multiple_of((by * BY + 2 * pair) * LANES, LANES), 2 * LANES)
            total = terms[:, at]
            low = total[8:24] + ehalo[0:16, at].astype(F32)
            high = total[48:64] + ehalo[16:32, at].astype(F32)
            third = jnp.maximum(
                jnp.concatenate([total[0:8], low, total[24:48], high, total[64:72]], axis=0), 0.0
            )
            one = third.astype(BF16).astype(F32)
            rest = third - one
            two = rest.astype(BF16).astype(F32)
            three = rest - two
            split = jnp.concatenate([one, two, three], axis=0).astype(BF16)
            logits = jnp.dot(wa_ref[...], split, preferred_element_type=F32)
            affinity = 1.0 / (1.0 + jnp.exp(-logits))
            for row in range(2):
                tile = affinity[:, row * LANES : (row + 1) * LANES]
                stacked = jnp.concatenate([tile] * nbx, axis=0)
                parts.append(jnp.where(block_mask, stacked, 0.0).astype(BF16))
        spread_out = jnp.concatenate(parts, axis=1)
        rows = nbx * ROWS
        tiles[pl.ds(pl.multiple_of(by * rows, rows), rows), :] = jnp.dot(
            spread_out, spread, preferred_element_type=F32
        ).astype(BF16)
        return 0

    lax.fori_loop(0, ny // BY, head, 0)

    count = tissue_ref.shape[1]
    blocks = (ny // BY) * nbx
    shape = (count, count)
    r = lax.broadcasted_iota(jnp.int32, shape, 0)
    c = lax.broadcasted_iota(jnp.int32, shape, 1)
    own_row = jnp.broadcast_to(owners_ref[...], shape)
    tis_row = jnp.broadcast_to(tissue_ref[...], shape)
    own_col = jnp.sum(jnp.where(r == c, own_row, 0), axis=1, keepdims=True)
    tis_col = jnp.sum(jnp.where(r == c, tis_row, 0), axis=1, keepdims=True)
    rank = jnp.sum(jnp.where((own_row == own_col) & (c < r), 1, 0), axis=1, keepdims=True)
    slot_col = own_col * SEND_CAP + rank
    wide_shape = (count, blocks * ROWS)
    block_of = lax.broadcasted_iota(jnp.int32, wide_shape, 1) // ROWS
    slot_row = (
        jnp.sum(jnp.where(tis_col == block_of, slot_col + 1, 0), axis=0, keepdims=True) - 1
    )

    group = 256

    def route(g, _):
        row = lax.broadcasted_iota(jnp.int32, (group, blocks * ROWS), 0) + g * group
        col = lax.broadcasted_iota(jnp.int32, (group, blocks * ROWS), 1)
        pick = (row // ROWS == slot_row) & (lax.rem(row, ROWS) == lax.rem(col, ROWS))
        pick = jnp.where(pick, 1.0, 0.0).astype(BF16)
        outgoing[pl.ds(pl.multiple_of(g * group, group), group), :] = jnp.dot(
            pick, tiles[...], preferred_element_type=F32
        ).astype(BF16)
        return 0

    lax.fori_loop(0, n * SEND_CAP * ROWS // group, route, 0)

    per = SEND_CAP * ROWS

    def message(step):
        target = lax.rem(me + step, n)
        return remote(
            outgoing.at[pl.ds(pl.multiple_of(target * per, per), per)],
            out_ref.at[me], asend.at[step], arecv.at[step], target,
        )

    def send(step, _):
        message(step).start()
        return 0

    def receive(step, _):
        message(step).wait()
        return 0

    lax.fori_loop(1, n, send, 0)
    out_ref[me] = outgoing[pl.ds(pl.multiple_of(me * per, per), per), :]
    lax.fori_loop(1, n, receive, 0)


def banded_weights(w_first, w_second, w_merge, w_affine, depth):
    c1, c0 = w_first.shape[0], w_first.shape[1] // 27
    c2 = w_second.shape[0]
    cu = w_merge.shape[0]
    zero = jnp.zeros((), BF16)

    def by_offset(w, channels):
        out = w.shape[0]
        return w.reshape(out, 3, 9, channels).transpose(0, 2, 1, 3).reshape(out, 9, 3 * channels)

    one = by_offset(w_first, c0)
    first = jnp.stack(
        [
            lax.pad(one, zero, ((0, 0, 0), (0, 0, 0), (4 + c0 * z, 80 - 4 - c0 * z - 3 * c0, 0)))
            for z in range(depth)
        ]
    ).reshape(depth * c1, 9 * 80)
    two = by_offset(w_second, c1)
    half = depth // 2
    second = jnp.stack(
        [
            lax.pad(two, zero, ((0, 0, 0), (0, 0, 0), (c1 * z, c1 * (half - 1 - z), 0)))
            for z in range(half)
        ]
    ).reshape(half * c2, 9 * (half + 2) * c1)
    three = (
        w_merge.reshape(cu, 3, 3, 3, c1).transpose(3, 0, 2, 1, 4).reshape(3, cu, 3, 3 * c1)
    )
    none = (0, 0, 0)
    third = jnp.stack(
        [
            lax.pad(three, zero, (none, none, none, (c1 * zo - 2 * c1, c1 * (depth + 1 - zo) - 2 * c1, 0)))
            for zo in range(depth + 2)
        ],
        axis=1,
    ).reshape(3 * (depth + 2) * cu, 3 * depth * c1)
    aff = w_affine.shape[0]
    place = jnp.eye(depth, depth + 2, 1, dtype=BF16)
    heads = (w_affine[:, None, None, :] * place[None, :, :, None]).reshape(
        aff * depth, (depth + 2) * cu
    )
    heads = jnp.pad(jnp.concatenate([heads] * 3, axis=1), ((0, ROWS - aff * depth), (0, 0)))
    return first, second, third, heads


def on_device(features, w_first, w_second, w_lift, w_merge, w_affine, tissue, owners):
    n = lax.axis_size("gz")
    channels, depth, ny, nx = features.shape
    cells = ny * nx
    hcells = (ny // 2) * nx
    flat = features.transpose(1, 0, 2, 3).reshape(depth * channels, cells)
    first, second, third, heads = banded_weights(w_first, w_second, w_merge, w_affine, depth)
    per = SEND_CAP * ROWS
    blocks = (ny // BY) * (nx // BX)
    vmem = pl.BlockSpec(memory_space=pltpu.VMEM)
    routed = pl.pallas_call(
        functools.partial(kernel, n, ny),
        out_shape=jax.ShapeDtypeStruct((n, per, LANES), BF16),
        in_specs=[vmem] * 8,
        out_specs=vmem,
        scratch_shapes=[
            pltpu.VMEM((32, cells), BF16),
            pltpu.VMEM((240, cells + 2 * LANES), BF16),
            pltpu.VMEM((192, cells), BF16),
            pltpu.VMEM((576, hcells + 2 * LANES), BF16),
            pltpu.VMEM((192, cells + 2 * LANES), BF16),
            pltpu.VMEM((72, cells), F32),
            pltpu.VMEM((32, cells), BF16),
            pltpu.VMEM((32, cells), BF16),
            pltpu.VMEM((blocks * ROWS, LANES), BF16),
            pltpu.VMEM((n * per, LANES), BF16),
            pltpu.SemaphoreType.DMA((2,)),
            pltpu.SemaphoreType.DMA((2,)),
            pltpu.SemaphoreType.DMA((2,)),
            pltpu.SemaphoreType.DMA((2,)),
            pltpu.SemaphoreType.DMA((2,)),
            pltpu.SemaphoreType.DMA((2,)),
            pltpu.SemaphoreType.DMA((n,)),
            pltpu.SemaphoreType.DMA((n,)),
        ],
        compiler_params=pltpu.CompilerParams(
            collective_id=0, has_side_effects=True, vmem_limit_bytes=48 * 1024 * 1024
        ),
        cost_estimate=pl.CostEstimate(
            flops=1600000000, bytes_accessed=2000000, transcendentals=65536
        ),
    )(flat, first, second, w_lift, third, heads, tissue, owners)
    used = w_affine.shape[0] * depth
    return routed.reshape(n, SEND_CAP, ROWS, LANES)[:, :, :used].reshape(
        1, n, SEND_CAP, used * LANES
    )


def solution(mesh):
    placed = (
        P(None, ("grp", "gz"), None, None),
        P(),
        P(),
        P(),
        P(),
        P(),
        P(("grp", "gz"), None),
        P(("grp", "gz"), None),
    )
    return jax.shard_map(
        on_device,
        mesh=mesh,
        in_specs=placed,
        out_specs=P(("grp", "gz"), None, None, None),
        check_vma=False,
    )
```

time: 168 us -> 50.2 us (0.30)
  local copies, waits for them, and re-layouts: 57.6 us -> 8.32 us
  Pallas kernels: 0 us -> 40.9 us
  matrix products: 35.7 us -> 0 us
  loops' own time: 20.7 us -> 0 us
  starting transfers between devices: 19.2 us -> 0 us
  blocking collectives: 14.8 us -> 0 us
  other arithmetic: 14.1 us -> 0.64 us
  waiting for transfers between devices: 4.06 us -> 0 us
    pallas_call x0 -> x1, Pallas kernels: none -> 40.9 us  [on_device(): pl.pallas_call(functools.partial(kernel, n, ny), out_shape=jax.ShapeDtype...]
    dot_general x99 -> x0, matrix products: 35.7 us -> none  [the longest x96 34 us: plane_terms(): jnp.einsum('oi,iyx->oyx', weight_part, stacked, preferred_element_type=jn...]
    another operation x3 -> x0, loops' own time: 20.7 us -> none  [convolve(): planes = lax.map(one_plane, jnp.arange(out_depth, dtype=jnp.int32))]
    ppermute x6 -> x0, starting transfers between devices: 19.2 us -> none  [the longest x3 15 us: padded_2(): lax.ppermute(tail, axis, [(i, (i + 1) % count) for i in range(ends)])]
    slice x25 -> x0, local copies, waits for them, and re-layouts: 18.2 us -> none  [the longest x22 18.1 us: plane_terms(): padded_plane[:, offset_y:offset_y + rows, offset_x:offset_x + columns]]
    all_to_all x1 -> x0, blocking collectives: 14.8 us -> none  [on_device(): lax.all_to_all(outgoing, 'gz', split_axis=0, concat_axis=0, tiled=True)]
    reduce_max x1 -> x0, other arithmetic: 8.37 us -> none  [maxpool(): volume.reshape(shape[0], shape[1] // 2, 2, shape[2] // 2, 2, shape[3] //...]
    squeeze x11 -> x0, local copies, waits for them, and re-layouts: 7.76 us -> none  [the longest x10 7.71 us: one_plane(): window_planes[:, 2]]
  transfers between devices with their start and end apart: 6 -> 0, of which waited for: 2 -> 0; matrix products, arithmetic and copies ran while one was open for 23% -> 0% of each run, Pallas kernels for 0% -> 0%
where the time goes in v1:
time: 50.2 us; the launch traced here: 50.1 us
  Pallas kernels  40.9 us (81%)
  local copies, waits for them, and re-layouts  8.32 us (17%)
  other arithmetic  0.64 us (1%)
    pallas_call x1, Pallas kernels, on_device(): pl.pallas_call(functools.partial(kernel, n, ny), out_shape=jax.ShapeDtype...  40.9 us
    reshape x2, local copies, waits for them, and re-layouts, banded_weights(): second = jnp.stack([lax.pad(two, zero, ((0, 0, 0), (0, 0, 0), (c1 * z, c1...  3.34 us
    unnamed x22, local copies, waits for them, and re-layouts  1.1 us
    reshape x2, local copies, waits for them, and re-layouts, banded_weights(): w_merge.reshape(cu, 3, 3, 3, c1).transpose(3, 0, 2, 1, 4)  1.07 us

profile of v1, /device:TPU:0, one launch (start us, length us, event | category | flops | bytes accessed | tf_op | source)
XLA Modules:
  0.0 50.1 jit_solution(15249904454391649408)
XLA Ops:
  0.0 0.0 copy-start.5
  0.0 0.9 %reshape.65 = bf16[12,3,3,3,48]{4,3,2,1,0:T(4,128)(2,1)S(1)} reshape(bf16[12,1296]{1,0:T(8,128)(2,1)} %param.12) | data formatting | bytes 62208 | tf_op jit(solution)/shard_map/reshape | solution.py:360
  1.0 0.1 reshape.66
  1.1 0.1 fusion.1
  1.3 0.1 bitcast_dynamic-update-slice_fusion.3
  1.4 0.1 bitcast_dynamic-update-slice_fusion.2
  1.5 0.1 bitcast_dynamic-update-slice_fusion.1
  1.6 0.1 bitcast_dynamic-update-slice_fusion
  1.7 0.1 fusion.3
  1.8 0.3 reshape.67.w3_ref
  2.1 0.0 copy-done.5
  2.2 0.1 copy.19
  2.4 0.1 pad_bitcast_fusion.5
  2.5 0.2 pad_maximum_fusion.1
  2.7 0.0 copy-start.4
  2.7 0.6 %copy.21 = bf16[4,48,9,80]{3,2,1,0:T(8,128)(2,1)S(1)} copy(bf16[4,48,9,80]{1,3,2,0:T(8,128)(2,1)S(1)} %pad_maximum_fusion.1) | data formatting | bytes 552960 | tf_op jit(solution)/shard_map/stack | solution.py:345
  3.4 0.5 %reshape.61.w1_ref = bf16[192,720]{1,0:T(8,128)(2,1)S(1)} reshape(bf16[4,48,9,80]{3,2,1,0:T(8,128)(2,1)S(1)} %copy.21) | data formatting | bytes 552960 | tf_op jit(solution)/shard_map/reshape | solution.py:350
  3.9 0.0 copy-done.4
  3.9 0.2 copy.22
  4.2 0.1 pad_bitcast_fusion.1
  4.3 0.2 pad_maximum_fusion
  4.5 2.2 %copy.34 = bf16[2,96,9,192]{3,2,1,0:T(8,128)(2,1)S(1)} copy(bf16[2,96,9,192]{1,3,2,0:T(8,128)(2,1)S(1)} %pad_maximum_fusion) | data formatting | bytes 1327104 | tf_op jit(solution)/shard_map/reshape | solution.py:358
  6.8 0.0 copy-start.3
  6.8 0.0 copy-start.6
  6.8 0.0 copy-start
  6.8 0.0 copy-start.1
  6.8 0.0 copy-start.2
  6.8 1.1 %reshape.70.w2_ref = bf16[192,1728]{1,0:T(8,128)(2,1)S(1)} reshape(bf16[2,96,9,192]{3,2,1,0:T(8,128)(2,1)S(1)} %copy.34) | data formatting | bytes 1327104 | tf_op jit(solution)/shard_map/reshape | solution.py:358
  7.9 0.0 copy-done.3
  8.0 0.2 copy.40
  8.1 0.1 fusion.9
  8.2 0.0 copy-done.6
  8.2 0.1 broadcast_multiply_fusion
  8.3 0.1 mul.20
  8.4 0.1 fusion.8.wa_ref
  8.5 0.0 copy-done
  8.5 0.0 copy-done.1
  8.5 0.0 copy-done.2
  8.5 40.9 %shard_map.82 = bf16[16,32,128]{2,1,0:T(8,128)(2,1)S(1)} custom-call(bf16[48,4096]{1,0:T(8,128)(2,1)S(1)} %bitcast.56, bf16[192,720]{1,0:T(8,128)(2,1)S(1)} %reshape.61.w1_ref, bf16[192,1728]{1,0:T(8,128)(2,1)S(1)} %reshape.70.w2_ref, bf16[48,96]{1,0:T(8,128)(2,1)S(1)} %copy-done, bf16[216,576]{1,0:T(8,128)(2,1)S(1)} %reshape.67.w3_ref, ...), custom_call_target="tpu_custom_call" | custom-call | flops 1600000000 | bytes 2000000 | tf_op jit(solution)/shard_map/pallas_call | solution.py:389
  49.4 0.7 %reshape.71 = bf16[1,16,2,1536]{3,2,1,0:T(2,128)(2,1)} reshape(bf16[16,2,12,128]{3,2,1,0:T(8,128)(2,1)S(1)} %bitcast.57) | data formatting | bytes 196608 | tf_op jit(solution)/shard_map/reshape | solution.py:422
  (7 shorter events, 0.2 us)
Async XLA Ops:
  0.0 2.2 %copy-start.5 = (bf16[48,324]{1,0:T(8,128)(2,1)S(1)}, bf16[48,324]{1,0:T(8,128)(2,1)}, u32[]{:S(2)}) copy-start(bf16[48,324]{1,0:T(8,128)(2,1)} %param.9) | copy-start | bytes 93316
  2.7 1.2 %copy-start.4 = (bf16[96,1296]{1,0:T(8,128)(2,1)S(1)}, bf16[96,1296]{1,0:T(8,128)(2,1)}, u32[]{:S(2)}) copy-start(bf16[96,1296]{1,0:T(8,128)(2,1)} %param.10) | copy-start | bytes 746500
  6.8 1.2 %copy-start.3 = (bf16[12,4,32,128]{3,2,1,0:T(8,128)(2,1)S(1)}, bf16[12,4,32,128]{3,2,1,0:T(8,128)(2,1)}, u32[]{:S(2)}) copy-start(bf16[12,4,32,128]{3,2,1,0:T(8,128)(2,1)} %param.8) | copy-start | bytes 1179652
  6.8 1.4 %copy-start.6 = (bf16[3,12]{1,0:T(4,128)(2,1)S(1)}, bf16[3,12]{1,0:T(4,128)(2,1)}, u32[]{:S(2)}) copy-start(bf16[3,12]{1,0:T(4,128)(2,1)} %param.13) | copy-start | bytes 220
  6.8 1.7 %copy-start = (bf16[48,96]{1,0:T(8,128)(2,1)S(1)}, bf16[48,96]{1,0:T(8,128)(2,1)}, u32[]{:S(2)}) copy-start(bf16[48,96]{1,0:T(8,128)(2,1)} %wl_ref.1) | copy-start | bytes 27652
  6.8 1.7 %copy-start.1 = (s32[1,32]{1,0:T(1,128)S(1)}, s32[1,32]{1,0:T(1,128)}, u32[]{:S(2)}) copy-start(s32[1,32]{1,0:T(1,128)} %tissue_ref.1) | copy-start | bytes 388
  6.8 1.7 %copy-start.2 = (s32[1,32]{1,0:T(1,128)S(1)}, s32[1,32]{1,0:T(1,128)}, u32[]{:S(2)}) copy-start(s32[1,32]{1,0:T(1,128)} %owners_ref.1) | copy-start | bytes 388

commit v2 on v1

v2 whole, which is shorter than its diff:
```python
import functools

import jax
import jax.numpy as jnp
import ml_dtypes
import numpy as np
from jax import lax
from jax.experimental import pallas as pl
from jax.experimental.pallas import tpu as pltpu
from jax.sharding import PartitionSpec as P

BY = 8
BX = 16
SEND_CAP = 2
LANES = 128
PART = 8
SEGS = 4
F32 = jnp.float32
BF16 = jnp.bfloat16


def lane_shift(tile, step, lane):
    rolled = pltpu.roll(tile, step % LANES, axis=1)
    keep = lane >= step if step > 0 else lane < LANES + step
    return jnp.where(keep, rolled, 0.0)


def kernel(
    n, ny,
    f_ref, w1_ref, w2_ref, wl_ref, w3_ref, wa_ref, tissue_ref, owners_ref,
    out_ref,
    fhalo, xpad, fmap, pool, mpad, terms, edge, ehalo, w2_band, picks, tiles, outgoing,
    fsend, frecv, psend, precv, esend, erecv, asend, arecv,
):
    me = lax.axis_index("gz")
    has_left = me > 0
    has_right = me < n - 1
    left = me - 1
    right = me + 1
    cells = ny * LANES
    hy = ny // 2
    hcells = hy * LANES

    barrier = pltpu.get_barrier_semaphore()

    def greet(step, _):
        pl.semaphore_signal(
            barrier, inc=1, device_id={"gz": lax.rem(me + step, n)},
            device_id_type=pl.DeviceIdType.MESH,
        )
        return 0

    lax.fori_loop(1, n, greet, 0)

    def lanes_of(rows):
        return lax.broadcasted_iota(jnp.int32, (rows, LANES), 1)

    xpad[:, 0:LANES] = jnp.zeros((240, LANES), BF16)
    xpad[:, cells + LANES : cells + 2 * LANES] = jnp.zeros((240, LANES), BF16)
    pool[:, 0:LANES] = jnp.zeros((576, LANES), BF16)
    pool[:, hcells + LANES : hcells + 2 * LANES] = jnp.zeros((576, LANES), BF16)
    mpad[:, 0:LANES] = jnp.zeros((192, LANES), BF16)
    mpad[:, cells + LANES : cells + 2 * LANES] = jnp.zeros((192, LANES), BF16)

    def remote(src, dst, send, recv, target):
        return pltpu.make_async_remote_copy(
            src_ref=src, dst_ref=dst, send_sem=send, recv_sem=recv,
            device_id={"gz": target}, device_id_type=pl.DeviceIdType.MESH,
        )

    def exchange(to_left, at_right, to_right, at_left, send, recv, seg):
        go_left = remote(to_left, at_right, send.at[0, seg], recv.at[0, seg], left)
        go_right = remote(to_right, at_left, send.at[1, seg], recv.at[1, seg], right)

        def start():
            @pl.when(has_left)
            def _():
                go_left.start()

            @pl.when(has_right)
            def _():
                go_right.start()

        def receive():
            @pl.when(has_right)
            def _():
                go_left.wait_recv()

            @pl.when(has_left)
            def _():
                go_right.wait_recv()

            @pl.when(jnp.logical_not(has_right))
            def _():
                at_right[...] = jnp.zeros(at_right.shape, at_right.dtype)

            @pl.when(jnp.logical_not(has_left))
            def _():
                at_left[...] = jnp.zeros(at_left.shape, at_left.dtype)

        def sent():
            @pl.when(has_left)
            def _():
                go_left.wait_send()

            @pl.when(has_right)
            def _():
                go_right.wait_send()

        return start, receive, sent

    pl.semaphore_wait(barrier, n - 1)

    features_start, features_receive, features_sent = exchange(
        f_ref.at[0:16], fhalo.at[16:32], f_ref.at[32:48], fhalo.at[0:16], fsend, frecv, 0
    )
    features_start()

    nbx = LANES // BX
    count = tissue_ref.shape[1]
    blocks = (ny // BY) * nbx
    shape = (count, count)
    r = lax.broadcasted_iota(jnp.int32, shape, 0)
    c = lax.broadcasted_iota(jnp.int32, shape, 1)
    own_row = jnp.broadcast_to(owners_ref[...], shape)
    tis_row = jnp.broadcast_to(tissue_ref[...], shape)
    own_col = jnp.sum(jnp.where(r == c, own_row, 0), axis=1, keepdims=True)
    tis_col = jnp.sum(jnp.where(r == c, tis_row, 0), axis=1, keepdims=True)
    rank = jnp.sum(jnp.where((own_row == own_col) & (c < r), 1, 0), axis=1, keepdims=True)
    slot_col = own_col * SEND_CAP + rank
    wide_shape = (count, blocks * PART)
    block_of = lax.broadcasted_iota(jnp.int32, wide_shape, 1) // PART
    slot_row = (
        jnp.sum(jnp.where(tis_col == block_of, slot_col + 1, 0), axis=0, keepdims=True) - 1
    )
    group = 256

    def pick_rows(g, _):
        row = lax.broadcasted_iota(jnp.int32, (group, blocks * PART), 0) + g * group
        col = lax.broadcasted_iota(jnp.int32, (group, blocks * PART), 1)
        pick = (row // PART == slot_row) & (lax.rem(row, PART) == lax.rem(col, PART))
        picks[pl.ds(pl.multiple_of(g * group, group), group), :] = jnp.where(
            pick, 1.0, 0.0
        ).astype(BF16)
        return 0

    groups = n * SEND_CAP * PART // group
    lax.fori_loop(0, groups, pick_rows, 0)

    w2 = w2_ref[...].astype(F32)
    blank = jnp.zeros((96, 432), F32)
    w2_band[0:96, :] = jnp.concatenate([w2, blank], axis=1).astype(BF16)
    w2_band[96:192, :] = jnp.concatenate([blank, w2], axis=1).astype(BF16)

    features_receive()

    def shift_features(y, _):
        at = pl.ds(pl.multiple_of(y * LANES, LANES), LANES)
        to = pl.ds(pl.multiple_of((y + 1) * LANES, LANES), LANES)
        lane = lanes_of(80)
        v = jnp.concatenate([fhalo[0:16, at], f_ref[:, at], fhalo[16:32, at]], axis=0)
        vf = v.astype(F32)
        xpad[0:80, to] = lane_shift(vf, 1, lane).astype(BF16)
        xpad[80:160, to] = v
        xpad[160:240, to] = lane_shift(vf, -1, lane).astype(BF16)
        return 0

    lax.fori_loop(0, ny, shift_features, 0, unroll=2)

    def shift_pool(row0, rows, v, to):
        lane = lanes_of(rows)
        pool[row0 : row0 + rows, to] = lane_shift(v, 2, lane).astype(BF16)
        pool[384 + row0 : 384 + row0 + rows, to] = lane_shift(v, -2, lane).astype(BF16)

    def first_conv(i, _):
        base = pl.multiple_of(i * 2 * LANES, 2 * LANES)
        patch = jnp.concatenate(
            [
                xpad[:, pl.ds(pl.multiple_of(base + b * LANES, LANES), 2 * LANES)]
                for b in range(3)
            ],
            axis=0,
        )
        acc = jnp.maximum(jnp.dot(w1_ref[...], patch, preferred_element_type=F32), 0.0)
        fmap[:, pl.ds(base, 2 * LANES)] = acc.astype(BF16)
        deep = jnp.concatenate(
            [jnp.maximum(acc[0:48], acc[48:96]), jnp.maximum(acc[96:144], acc[144:192])], axis=0
        )
        wide = jnp.maximum(deep[:, 0:LANES], deep[:, LANES : 2 * LANES])
        even = lax.rem(lanes_of(96), 2) == 0
        other = jnp.where(
            even, pltpu.roll(wide, LANES - 1, axis=1), pltpu.roll(wide, 1, axis=1)
        )
        both = jnp.maximum(wide, other)
        to = pl.ds(pl.multiple_of((i + 1) * LANES, LANES), LANES)
        pool[240:336, to] = both.astype(BF16)
        shift_pool(48, 96, both, to)
        return 0

    seg_rows = hy // SEGS

    def pooled(seg):
        at = pl.ds(pl.multiple_of((seg * seg_rows + 1) * LANES, LANES), seg_rows * LANES)
        return exchange(
            pool.at[240:288, at], pool.at[336:384, at],
            pool.at[288:336, at], pool.at[192:240, at], psend, precv, seg,
        )

    def first_segment(seg, _):
        lax.fori_loop(
            0, seg_rows, lambda i, _: first_conv(seg * seg_rows + i, 0), 0, unroll=2
        )
        pooled(seg)[0]()
        return 0

    lax.fori_loop(0, SEGS, first_segment, 0)

    def shift_halo(y, _):
        to = pl.ds(pl.multiple_of((y + 1) * LANES, LANES), LANES)
        shift_pool(0, 48, pool[192:240, to].astype(F32), to)
        shift_pool(144, 48, pool[336:384, to].astype(F32), to)
        return 0

    def second_conv(i, _):
        base = pl.multiple_of(i * 2 * LANES, 2 * LANES)
        patch = jnp.concatenate(
            [
                pool[
                    192 * c + 48 * plane : 192 * c + 48 * plane + 48,
                    pl.ds(pl.multiple_of(base + b * LANES, LANES), 2 * LANES),
                ]
                for plane in range(4)
                for b in range(3)
                for c in range(3)
            ],
            axis=0,
        )
        acc = jnp.dot(w2_band[...], patch, preferred_element_type=F32)
        second = jnp.maximum(acc, 0.0).astype(BF16)
        for half in range(2):
            lifted = jnp.dot(
                wl_ref[...], second[96 * half : 96 * half + 96], preferred_element_type=F32
            )
            for row in range(4):
                part = lifted[:, (row // 2) * LANES : (row // 2 + 1) * LANES]
                for deep in range(2):
                    plane = 48 * (2 * half + deep)
                    own = fmap[
                        plane : plane + 48,
                        pl.ds(pl.multiple_of(i * 4 * LANES + row * LANES, LANES), LANES),
                    ]
                    mpad[
                        plane : plane + 48,
                        pl.ds(pl.multiple_of(i * 4 * LANES + (row + 1) * LANES, LANES), LANES),
                    ] = (part + own.astype(F32)).astype(BF16)
        return 0

    per_seg = seg_rows // 2
    for seg in range(SEGS):
        pooled(seg)[1]()
        lax.fori_loop(seg * seg_rows, (seg + 1) * seg_rows, shift_halo, 0, unroll=2)
        first = max(seg * per_seg - 1, 0)
        last = (seg + 1) * per_seg - (0 if seg == SEGS - 1 else 1)
        lax.fori_loop(first, last, second_conv, 0)

    def third_conv(i, _):
        base = pl.multiple_of(i * 2 * LANES, 2 * LANES)
        patch = jnp.concatenate(
            [
                mpad[:, pl.ds(pl.multiple_of(base + b * LANES, LANES), 2 * LANES)]
                for b in range(3)
            ],
            axis=0,
        )
        acc = jnp.dot(w3_ref[...], patch, preferred_element_type=F32)
        lane = lanes_of(72)
        for row in range(2):
            at = slice(row * LANES, (row + 1) * LANES)
            total = (
                acc[72:144, at]
                + lane_shift(acc[0:72, at], 1, lane)
                + lane_shift(acc[144:216, at], -1, lane)
            )
            to = pl.ds(pl.multiple_of(base + row * LANES, LANES), LANES)
            terms[:, to] = total
            edge[0:16, to] = total[0:16].astype(BF16)
            edge[16:32, to] = total[56:72].astype(BF16)
        return 0

    def edges(seg):
        at = pl.ds(pl.multiple_of(seg * BY * LANES, BY * LANES), BY * LANES)
        return exchange(
            edge.at[0:16, at], ehalo.at[16:32, at],
            edge.at[16:32, at], ehalo.at[0:16, at], esend, erecv, seg,
        )

    def third_segment(seg, _):
        lax.fori_loop(
            0, BY // 2, lambda i, _: third_conv(seg * (BY // 2) + i, 0), 0, unroll=2
        )
        edges(seg)[0]()
        return 0

    lax.fori_loop(0, ny // BY, third_segment, 0)

    spread_row = lax.broadcasted_iota(jnp.int32, (BY * LANES, LANES), 0)
    spread_col = lax.broadcasted_iota(jnp.int32, (BY * LANES, LANES), 1)
    spread = jnp.where(
        spread_col == (spread_row // LANES) * BX + lax.rem(spread_row, BX), 1.0, 0.0
    ).astype(BF16)
    block_mask = (
        lax.broadcasted_iota(jnp.int32, (nbx * PART, LANES), 0) // PART
        == lax.broadcasted_iota(jnp.int32, (nbx * PART, LANES), 1) // BX
    )
    directions, channels = wa_ref.shape

    def head_matrix(rows, first_at, second_at):
        across = 3 * rows
        inside = lax.rem(lax.broadcasted_iota(jnp.int32, (channels, across), 1), rows)
        channel = lax.broadcasted_iota(jnp.int32, (channels, across), 0)
        hit = (inside == channel + first_at) | (inside == channel + second_at)
        columns = jnp.dot(
            wa_ref[...], jnp.where(hit, 1.0, 0.0).astype(BF16), preferred_element_type=F32
        ).astype(BF16)
        turn = lax.broadcasted_iota(jnp.int32, (PART, directions), 0) // 2
        turn = turn == lax.broadcasted_iota(jnp.int32, (PART, directions), 1)
        full = jnp.dot(
            jnp.where(turn, 1.0, 0.0).astype(BF16), columns, preferred_element_type=F32
        )
        at = lax.rem(lax.broadcasted_iota(jnp.int32, (PART, across), 1), rows)
        odd = lax.rem(lax.broadcasted_iota(jnp.int32, (PART, across), 0), 2) == 1
        start = jnp.where(odd, second_at, first_at)
        keep = (at >= start) & (at < start + channels)
        return jnp.where(keep, full, 0.0).astype(BF16)

    def head_rows(matrix, part, total_of):
        def head(by, _):
            parts = []
            for pair in range(BY // 2):
                at = pl.ds(pl.multiple_of((by * BY + 2 * pair) * LANES, LANES), 2 * LANES)
                third = jnp.maximum(total_of(at), 0.0)
                one = third.astype(BF16).astype(F32)
                rest = third - one
                two = rest.astype(BF16).astype(F32)
                three = rest - two
                split = jnp.concatenate([one, two, three], axis=0).astype(BF16)
                logits = jnp.dot(matrix, split, preferred_element_type=F32)
                affinity = 1.0 / (1.0 + jnp.exp(-logits))
                for row in range(2):
                    tile = affinity[:, row * LANES : (row + 1) * LANES]
                    stacked = jnp.concatenate([tile] * nbx, axis=0)
                    parts.append(jnp.where(block_mask, stacked, 0.0).astype(BF16))
            rows = nbx * PART
            tiles[part, pl.ds(pl.multiple_of(by * rows, rows), rows), :] = jnp.dot(
                jnp.concatenate(parts, axis=1), spread, preferred_element_type=F32
            ).astype(BF16)
            return 0

        return head

    per = SEND_CAP * PART

    def message(part, step):
        target = lax.rem(me + step, n)
        return remote(
            outgoing.at[part, pl.ds(pl.multiple_of(target * per, per), per)],
            out_ref.at[part, me], asend.at[part, step], arecv.at[part, step], target,
        )

    def send_part(part):
        def route(g, _):
            at = pl.ds(pl.multiple_of(g * group, group), group)
            outgoing[part, at, :] = jnp.dot(
                picks[at, :], tiles[part], preferred_element_type=F32
            ).astype(BF16)
            return 0

        def send(step, _):
            message(part, step).start()
            return 0

        lax.fori_loop(0, groups, route, 0)
        lax.fori_loop(1, n, send, 0)
        out_ref[part, me] = outgoing[part, pl.ds(pl.multiple_of(me * per, per), per), :]

    inner_head = head_rows(head_matrix(24, 0, 12), 0, lambda at: terms[24:48, at])
    lax.fori_loop(0, ny // BY, inner_head, 0)
    send_part(0)

    def outer_total(at):
        low = terms[8:24, at] + ehalo[0:16, at].astype(F32)
        high = terms[48:64, at] + ehalo[16:32, at].astype(F32)
        return jnp.concatenate([low, high], axis=0)

    outer_head = head_rows(head_matrix(32, 4, 16), 1, outer_total)

    def outer_segment(by, _):
        edges(by)[1]()
        return outer_head(by, 0)

    lax.fori_loop(0, ny // BY, outer_segment, 0)
    send_part(1)

    features_sent()

    def pooled_sent(seg, _):
        pooled(seg)[2]()
        return 0

    def edges_sent(seg, _):
        edges(seg)[2]()
        return 0

    lax.fori_loop(0, SEGS, pooled_sent, 0)
    lax.fori_loop(0, ny // BY, edges_sent, 0)

    def receive(step, _):
        message(0, step).wait()
        message(1, step).wait()
        return 0

    lax.fori_loop(1, n, receive, 0)


def banded_weights(w_first, w_merge, depth):
    c1, c0 = w_first.shape[0], w_first.shape[1] // 27
    cu = w_merge.shape[0]
    zero = jnp.zeros((), BF16)
    place = np.zeros((depth, 3, 9, c0, 9, 80), np.float32)
    for z in range(depth):
        for a in range(3):
            for i in range(c0):
                for bc in range(9):
                    place[z, a, bc, i, bc, 4 + c0 * (z + a) + i] = 1
    place = place.reshape(depth, 27 * c0, 720).astype(ml_dtypes.bfloat16)
    first = jnp.einsum("oi,zik->zok", w_first, place, preferred_element_type=F32)
    first = first.astype(BF16).reshape(depth * c1, 720)
    three = (
        w_merge.reshape(cu, 3, 3, 3, c1).transpose(3, 0, 2, 1, 4).reshape(3, cu, 3, 3 * c1)
    )
    none = (0, 0, 0)
    third = jnp.stack(
        [
            lax.pad(three, zero, (none, none, none, (c1 * zo - 2 * c1, c1 * (depth + 1 - zo) - 2 * c1, 0)))
            for zo in range(depth + 2)
        ],
        axis=1,
    ).reshape(3 * (depth + 2) * cu, 3 * depth * c1)
    return first, third


def on_device(features, w_first, w_second, w_lift, w_merge, w_affine, tissue, owners):
    n = lax.axis_size("gz")
    channels, depth, ny, nx = features.shape
    cells = ny * nx
    hcells = (ny // 2) * nx
    flat = features.transpose(1, 0, 2, 3).reshape(depth * channels, cells)
    first, third = banded_weights(w_first, w_merge, depth)
    per = SEND_CAP * PART
    blocks = (ny // BY) * (nx // BX)
    vmem = pl.BlockSpec(memory_space=pltpu.VMEM)
    routed = pl.pallas_call(
        functools.partial(kernel, n, ny),
        out_shape=jax.ShapeDtypeStruct((2, n, per, LANES), BF16),
        in_specs=[vmem] * 8,
        out_specs=vmem,
        scratch_shapes=[
            pltpu.VMEM((32, cells), BF16),
            pltpu.VMEM((240, cells + 2 * LANES), BF16),
            pltpu.VMEM((192, cells), BF16),
            pltpu.VMEM((576, hcells + 2 * LANES), BF16),
            pltpu.VMEM((192, cells + 2 * LANES), BF16),
            pltpu.VMEM((72, cells), F32),
            pltpu.VMEM((32, cells), BF16),
            pltpu.VMEM((32, cells), BF16),
            pltpu.VMEM((192, 1728), BF16),
            pltpu.VMEM((n * per, blocks * PART), BF16),
            pltpu.VMEM((2, blocks * PART, LANES), BF16),
            pltpu.VMEM((2, n * per, LANES), BF16),
            pltpu.SemaphoreType.DMA((2, 1)),
            pltpu.SemaphoreType.DMA((2, 1)),
            pltpu.SemaphoreType.DMA((2, SEGS)),
            pltpu.SemaphoreType.DMA((2, SEGS)),
            pltpu.SemaphoreType.DMA((2, ny // BY)),
            pltpu.SemaphoreType.DMA((2, ny // BY)),
            pltpu.SemaphoreType.DMA((2, n)),
            pltpu.SemaphoreType.DMA((2, n)),
        ],
        compiler_params=pltpu.CompilerParams(
            collective_id=0, has_side_effects=True, vmem_limit_bytes=48 * 1024 * 1024
        ),
        cost_estimate=pl.CostEstimate(
            flops=1600000000, bytes_accessed=2000000, transcendentals=65536
        ),
    )(flat, first, w_second, w_lift, third, w_affine, tissue, owners)
    directions = w_affine.shape[0]
    routed = routed.reshape(2, n, SEND_CAP, PART // 2, 2, LANES)[:, :, :, :directions]
    routed = jnp.concatenate(
        [routed[1, :, :, :, :1], routed[0], routed[1, :, :, :, 1:]], axis=3
    )
    return routed.reshape(1, n, SEND_CAP, directions * depth * LANES)


def solution(mesh):
    placed = (
        P(None, ("grp", "gz"), None, None),
        P(),
        P(),
        P(),
        P(),
        P(),
        P(("grp", "gz"), None),
        P(("grp", "gz"), None),
    )
    return jax.shard_map(
        on_device,
        mesh=mesh,
        in_specs=placed,
        out_specs=P(("grp", "gz"), None, None, None),
        check_vma=False,
    )
```

time: 50.2 us -> 39 us (0.78)
  Pallas kernels: 40.9 us -> 33.5 us
  local copies, waits for them, and re-layouts: 8.32 us -> 4.43 us
    pallas_call x1, Pallas kernels: 40.9 us -> 33.5 us  [on_device(): pl.pallas_call(functools.partial(kernel, n, ny), out_shape=jax.ShapeDtype...]
    reshape x6 -> x1, local copies, waits for them, and re-layouts: 4.6 us -> 0.67 us  [on_device(): return routed.reshape(1, n, SEND_CAP, directions * depth * LANES)]
    transpose x1, local copies, waits for them, and re-layouts: 0.03 us -> 1.11 us  [on_device(): flat = features.transpose(1, 0, 2, 3).reshape(depth * channels, cells)]
    another operation x3 -> x0, local copies, waits for them, and re-layouts: 0.9 us -> none  [the longest x2 0.76 us: banded_weights(): jnp.stack([lax.pad(one, zero, ((0, 0, 0), (0, 0, 0), (4 + c0 * z, 80 - 4...]
    unnamed x22 -> x20, local copies, waits for them, and re-layouts: 1.1 us -> 0.76 us
where the time goes in v2:
time: 39 us; the launch traced here: 38.8 us
  Pallas kernels  33.5 us (86%)
  local copies, waits for them, and re-layouts  4.43 us (11%)
  matrix products  0.49 us (1%)
    pallas_call x1, Pallas kernels, on_device(): pl.pallas_call(functools.partial(kernel, n, ny), out_shape=jax.ShapeDtype...  33.5 us
    reshape x2, local copies, waits for them, and re-layouts, banded_weights(): w_merge.reshape(cu, 3, 3, 3, c1).transpose(3, 0, 2, 1, 4)  1.21 us
    transpose x1, local copies, waits for them, and re-layouts, on_device(): flat = features.transpose(1, 0, 2, 3).reshape(depth * channels, cells)  1.11 us

profile of v2, /device:TPU:0, one launch (start us, length us, event | category | flops | bytes accessed | tf_op | source)
XLA Modules:
  0.0 38.8 jit_solution(5200725194902138571)
XLA Ops:
  0.0 0.0 copy-start
  0.0 0.0 copy-start.6
  0.0 1.1 %reshape.23 = bf16[12,3,3,3,48]{4,3,2,1,0:T(4,128)(2,1)S(1)} reshape(bf16[12,1296]{1,0:T(8,128)(2,1)} %param.13) | data formatting | bytes 62208 | tf_op jit(solution)/shard_map/reshape | solution.py:439
  1.1 0.1 reshape.24
  1.3 0.1 fusion.1
  1.4 0.1 bitcast_dynamic-update-slice_fusion.3
  1.5 0.1 bitcast_dynamic-update-slice_fusion.2
  1.6 0.1 bitcast_dynamic-update-slice_fusion.1
  1.7 0.1 bitcast_dynamic-update-slice_fusion
  1.8 0.1 fusion.3
  2.0 0.3 reshape.25.w3_ref
  2.3 0.0 copy-start.1
  2.3 0.0 copy-start.2
  2.3 0.0 copy-start.3
  2.3 0.0 copy-start.4
  2.3 0.0 copy-start.5
  2.4 1.1 %copy.19 = bf16[4,12,32,128]{3,2,1,0:T(8,128)(2,1)S(1)} copy(bf16[4,12,32,128]{3,2,0,1:T(8,128)(2,1)} %bitcast.53) | data formatting | bytes 786432 | tf_op jit(solution)/shard_map/transpose | solution.py:457
  3.5 0.2 copy.36
  3.6 0.0 copy-done
  3.6 0.0 copy-done.6
  3.7 0.5 %convolution_convert_fusion = bf16[4,720,48]{1,2,0:T(8,128)(2,1)S(1)} fusion(bf16[4,324,720]{2,1,0:T(8,128)(2,1)S(1)} %copy-done.6, bf16[48,324]{1,0:T(8,128)(2,1)S(1)} %copy-done), kind=kOutput, calls=%fused_computation | convolution fusion | flops 89717760 | bytes 2173824 | tf_op jit(solution)/shard_map/oi,zik->zok/dot_general | solution.py:436
  4.1 0.0 copy-done.1
  4.2 0.0 copy-done.2
  4.2 0.0 copy-done.3
  4.2 0.0 copy-done.4
  4.2 0.0 copy-done.5
  4.2 33.5 %shard_map.91 = bf16[2,16,16,128]{3,2,1,0:T(8,128)(2,1)S(1)} custom-call(bf16[48,4096]{1,0:T(8,128)(2,1)S(1)} %bitcast.47, bf16[192,720]{1,0:T(8,128)(2,1)S(1)} %bitcast.48, bf16[96,1296]{1,0:T(8,128)(2,1)S(1)} %copy-done.1, bf16[48,96]{1,0:T(8,128)(2,1)S(1)} %copy-done.2, bf16[216,576]{1,0:T(8,128)(2,1)S(1)} %reshape.25.w3_ref, ...), custom_call_target="tpu_custom_call" | custom-call | flops 1600000000 | bytes 2000000 | tf_op jit(solution)/shard_map/pallas_call | solution.py:462
  37.7 0.1 fusion.5
  38.0 0.2 pad_maximum_fusion
  38.1 0.7 %reshape.27 = bf16[1,16,2,1536]{3,2,1,0:T(2,128)(2,1)} reshape(bf16[16,2,3,4,128]{4,3,2,1,0:T(4,128)(2,1)S(1)} %pad_maximum_fusion) | data formatting | bytes 196608 | tf_op jit(solution)/shard_map/reshape | solution.py:501
  (5 shorter events, 0.2 us)
Async XLA Ops:
  0.0 3.6 %copy-start = (bf16[48,324]{1,0:T(8,128)(2,1)S(1)}, bf16[48,324]{1,0:T(8,128)(2,1)}, u32[]{:S(2)}) copy-start(bf16[48,324]{1,0:T(8,128)(2,1)} %param.10) | copy-start | bytes 93316
  0.0 3.6 %copy-start.6 = (bf16[4,324,720]{2,1,0:T(8,128)(2,1)S(1)}, bf16[4,324,720]{2,1,0:T(8,128)(2,1)}, u32[]{:S(2)}) copy-start(bf16[4,324,720]{2,1,0:T(8,128)(2,1)} %constant.4.clone) | copy-start | bytes 5598724
  2.3 1.9 %copy-start.1 = (bf16[96,1296]{1,0:T(8,128)(2,1)S(1)}, bf16[96,1296]{1,0:T(8,128)(2,1)}, u32[]{:S(2)}) copy-start(bf16[96,1296]{1,0:T(8,128)(2,1)} %w2_ref.1) | copy-start | bytes 746500
  2.3 1.9 %copy-start.2 = (bf16[48,96]{1,0:T(8,128)(2,1)S(1)}, bf16[48,96]{1,0:T(8,128)(2,1)}, u32[]{:S(2)}) copy-start(bf16[48,96]{1,0:T(8,128)(2,1)} %wl_ref.1) | copy-start | bytes 27652
  2.3 1.9 %copy-start.3 = (bf16[3,12]{1,0:T(4,128)(2,1)S(1)}, bf16[3,12]{1,0:T(4,128)(2,1)}, u32[]{:S(2)}) copy-start(bf16[3,12]{1,0:T(4,128)(2,1)} %wa_ref.1) | copy-start | bytes 220
  2.3 1.8 %copy-start.4 = (s32[1,32]{1,0:T(1,128)S(1)}, s32[1,32]{1,0:T(1,128)}, u32[]{:S(2)}) copy-start(s32[1,32]{1,0:T(1,128)} %tissue_ref.1) | copy-start | bytes 388
  2.3 1.8 %copy-start.5 = (s32[1,32]{1,0:T(1,128)S(1)}, s32[1,32]{1,0:T(1,128)}, u32[]{:S(2)}) copy-start(s32[1,32]{1,0:T(1,128)} %owners_ref.1) | copy-start | bytes 388

commit v3 on v2

--- a/solution.py
+++ b/solution.py
@@ -27,9 +27,9 @@
 
 def kernel(
     n, ny,
-    f_ref, w1_ref, w2_ref, wl_ref, w3_ref, wa_ref, tissue_ref, owners_ref,
+    f_ref, rim_ref, w1_ref, w2_ref, wl_ref, w3_ref, wa_ref, tissue_ref, owners_ref,
     out_ref,
-    fhalo, xpad, fmap, pool, mpad, terms, edge, ehalo, w2_band, picks, tiles, outgoing,
+    fhalo, xpad, fmap, pool, mpad, terms, edge, ehalo, w2_band, w3_band, picks, masked, tiles, outgoing,
     fsend, frecv, psend, precv, esend, erecv, asend, arecv,
 ):
     me = lax.axis_index("gz")
@@ -112,7 +112,7 @@
     pl.semaphore_wait(barrier, n - 1)
 
     features_start, features_receive, features_sent = exchange(
-        f_ref.at[0:16], fhalo.at[16:32], f_ref.at[32:48], fhalo.at[0:16], fsend, frecv, 0
+        rim_ref.at[0:16], fhalo.at[16:32], rim_ref.at[16:32], fhalo.at[0:16], fsend, frecv, 0
     )
     features_start()
 
@@ -152,20 +152,48 @@
     w2_band[0:96, :] = jnp.concatenate([w2, blank], axis=1).astype(BF16)
     w2_band[96:192, :] = jnp.concatenate([blank, w2], axis=1).astype(BF16)
 
-    features_receive()
-
-    def shift_features(y, _):
+    w3 = w3_ref[...].astype(F32)
+    bands = []
+    for c_off in range(3):
+        columns = jnp.concatenate(
+            [w3[:, (3 * ab + c_off) * 48 : (3 * ab + c_off) * 48 + 48] for ab in range(9)], axis=1
+        )
+        for zo in range(6):
+            first = 144 * (zo - 2)
+            low, high = max(first, 0), min(first + 432, 576)
+            pieces = [columns[:, low - first : high - first]]
+            if low > 0:
+                pieces.insert(0, jnp.zeros((12, low), F32))
+            if high < 576:
+                pieces.append(jnp.zeros((12, 576 - high), F32))
+            bands.append(jnp.concatenate(pieces, axis=1))
+    w3_band[...] = jnp.concatenate(bands, axis=0).astype(BF16)
+
+    def shift_rows(v, row0, to):
+        rows = v.shape[0]
+        lane = lanes_of(rows)
+        vf = v.astype(F32)
+        xpad[row0 : row0 + rows, to] = lane_shift(vf, 1, lane).astype(BF16)
+        xpad[80 + row0 : 80 + row0 + rows, to] = v
+        xpad[160 + row0 : 160 + row0 + rows, to] = lane_shift(vf, -1, lane).astype(BF16)
+
+    def shift_own(y, _):
         at = pl.ds(pl.multiple_of(y * LANES, LANES), LANES)
         to = pl.ds(pl.multiple_of((y + 1) * LANES, LANES), LANES)
-        lane = lanes_of(80)
-        v = jnp.concatenate([fhalo[0:16, at], f_ref[:, at], fhalo[16:32, at]], axis=0)
-        vf = v.astype(F32)
-        xpad[0:80, to] = lane_shift(vf, 1, lane).astype(BF16)
-        xpad[80:160, to] = v
-        xpad[160:240, to] = lane_shift(vf, -1, lane).astype(BF16)
-        return 0
-
-    lax.fori_loop(0, ny, shift_features, 0, unroll=2)
+        shift_rows(f_ref[:, at], 16, to)
+        return 0
+
+    lax.fori_loop(0, ny, shift_own, 0, unroll=4)
+    features_receive()
+
+    def shift_rims(y, _):
+        at = pl.ds(pl.multiple_of(y * LANES, LANES), LANES)
+        to = pl.ds(pl.multiple_of((y + 1) * LANES, LANES), LANES)
+        shift_rows(fhalo[0:16, at], 0, to)
+        shift_rows(fhalo[16:32, at], 64, to)
+        return 0
+
+    lax.fori_loop(0, ny, shift_rims, 0, unroll=4)
 
     def shift_pool(row0, rows, v, to):
         lane = lanes_of(rows)
@@ -208,7 +236,7 @@
 
     def first_segment(seg, _):
         lax.fori_loop(
-            0, seg_rows, lambda i, _: first_conv(seg * seg_rows + i, 0), 0, unroll=2
+            0, seg_rows, lambda i, _: first_conv(seg * seg_rows + i, 0), 0, unroll=True
         )
         pooled(seg)[0]()
         return 0
@@ -258,21 +286,25 @@
     per_seg = seg_rows // 2
     for seg in range(SEGS):
         pooled(seg)[1]()
-        lax.fori_loop(seg * seg_rows, (seg + 1) * seg_rows, shift_halo, 0, unroll=2)
+        lax.fori_loop(seg * seg_rows, (seg + 1) * seg_rows, shift_halo, 0, unroll=True)
         first = max(seg * per_seg - 1, 0)
         last = (seg + 1) * per_seg - (0 if seg == SEGS - 1 else 1)
-        lax.fori_loop(first, last, second_conv, 0)
+        lax.fori_loop(first, last, second_conv, 0, unroll=True)
 
     def third_conv(i, _):
         base = pl.multiple_of(i * 2 * LANES, 2 * LANES)
         patch = jnp.concatenate(
             [
-                mpad[:, pl.ds(pl.multiple_of(base + b * LANES, LANES), 2 * LANES)]
+                mpad[
+                    48 * plane : 48 * plane + 48,
+                    pl.ds(pl.multiple_of(base + b * LANES, LANES), 2 * LANES),
+                ]
+                for plane in range(4)
                 for b in range(3)
             ],
             axis=0,
         )
-        acc = jnp.dot(w3_ref[...], patch, preferred_element_type=F32)
+        acc = jnp.dot(w3_band[...], patch, preferred_element_type=F32)
         lane = lanes_of(72)
         for row in range(2):
             at = slice(row * LANES, (row + 1) * LANES)
@@ -296,7 +328,7 @@
 
     def third_segment(seg, _):
         lax.fori_loop(
-            0, BY // 2, lambda i, _: third_conv(seg * (BY // 2) + i, 0), 0, unroll=2
+            0, BY // 2, lambda i, _: third_conv(seg * (BY // 2) + i, 0), 0, unroll=True
         )
         edges(seg)[0]()
         return 0
@@ -333,7 +365,7 @@
         keep = (at >= start) & (at < start + channels)
         return jnp.where(keep, full, 0.0).astype(BF16)
 
-    def head_rows(matrix, part, total_of):
+    def head_rows(matrix, total_of):
         def head(by, _):
             parts = []
             for pair in range(BY // 2):
@@ -351,9 +383,9 @@
                     stacked = jnp.concatenate([tile] * nbx, axis=0)
                     parts.append(jnp.where(block_mask, stacked, 0.0).astype(BF16))
             rows = nbx * PART
-            tiles[part, pl.ds(pl.multiple_of(by * rows, rows), rows), :] = jnp.dot(
-                jnp.concatenate(parts, axis=1), spread, preferred_element_type=F32
-            ).astype(BF16)
+            masked[pl.ds(pl.multiple_of(by * rows, rows), rows), :] = jnp.concatenate(
+                parts, axis=1
+            )
             return 0
 
         return head
@@ -368,6 +400,8 @@
         )
 
     def send_part(part):
+        tiles[part] = jnp.dot(masked[...], spread, preferred_element_type=F32).astype(BF16)
+
         def route(g, _):
             at = pl.ds(pl.multiple_of(g * group, group), group)
             outgoing[part, at, :] = jnp.dot(
@@ -383,8 +417,8 @@
         lax.fori_loop(1, n, send, 0)
         out_ref[part, me] = outgoing[part, pl.ds(pl.multiple_of(me * per, per), per), :]
 
-    inner_head = head_rows(head_matrix(24, 0, 12), 0, lambda at: terms[24:48, at])
-    lax.fori_loop(0, ny // BY, inner_head, 0)
+    inner_head = head_rows(head_matrix(24, 0, 12), lambda at: terms[24:48, at])
+    lax.fori_loop(0, ny // BY, inner_head, 0, unroll=2)
     send_part(0)
 
     def outer_total(at):
@@ -392,7 +426,7 @@
         high = terms[48:64, at] + ehalo[16:32, at].astype(F32)
         return jnp.concatenate([low, high], axis=0)
 
-    outer_head = head_rows(head_matrix(32, 4, 16), 1, outer_total)
+    outer_head = head_rows(head_matrix(32, 4, 16), outer_total)
 
     def outer_segment(by, _):
         edges(by)[1]()
@@ -422,31 +456,24 @@
     lax.fori_loop(1, n, receive, 0)
 
 
-def banded_weights(w_first, w_merge, depth):
+def first_matrix(w_first, depth):
     c1, c0 = w_first.shape[0], w_first.shape[1] // 27
-    cu = w_merge.shape[0]
-    zero = jnp.zeros((), BF16)
     place = np.zeros((depth, 3, 9, c0, 9, 80), np.float32)
     for z in range(depth):
         for a in range(3):
             for i in range(c0):
+                plane = z + a - 1
+                if plane < 0:
+                    row = i
+                elif plane == depth:
+                    row = 64 + i
+                else:
+                    row = 16 + depth * i + plane
                 for bc in range(9):
-                    place[z, a, bc, i, bc, 4 + c0 * (z + a) + i] = 1
+                    place[z, a, bc, i, bc, row] = 1
     place = place.reshape(depth, 27 * c0, 720).astype(ml_dtypes.bfloat16)
     first = jnp.einsum("oi,zik->zok", w_first, place, preferred_element_type=F32)
-    first = first.astype(BF16).reshape(depth * c1, 720)
-    three = (
-        w_merge.reshape(cu, 3, 3, 3, c1).transpose(3, 0, 2, 1, 4).reshape(3, cu, 3, 3 * c1)
-    )
-    none = (0, 0, 0)
-    third = jnp.stack(
-        [
-            lax.pad(three, zero, (none, none, none, (c1 * zo - 2 * c1, c1 * (depth + 1 - zo) - 2 * c1, 0)))
-            for zo in range(depth + 2)
-        ],
-        axis=1,
-    ).reshape(3 * (depth + 2) * cu, 3 * depth * c1)
-    return first, third
+    return first.astype(BF16).reshape(depth * c1, 720)
 
 
 def on_device(features, w_first, w_second, w_lift, w_merge, w_affine, tissue, owners):
@@ -454,15 +481,17 @@
     channels, depth, ny, nx = features.shape
     cells = ny * nx
     hcells = (ny // 2) * nx
-    flat = features.transpose(1, 0, 2, 3).reshape(depth * channels, cells)
-    first, third = banded_weights(w_first, w_merge, depth)
+    flat = features.reshape(channels * depth, cells)
+    rims = jnp.stack([features[:, 0], features[:, depth - 1]])
+    rims = jnp.pad(rims, ((0, 0), (0, 16 - channels), (0, 0), (0, 0))).reshape(32, cells)
+    first = first_matrix(w_first, depth)
     per = SEND_CAP * PART
     blocks = (ny // BY) * (nx // BX)
     vmem = pl.BlockSpec(memory_space=pltpu.VMEM)
     routed = pl.pallas_call(
         functools.partial(kernel, n, ny),
         out_shape=jax.ShapeDtypeStruct((2, n, per, LANES), BF16),
-        in_specs=[vmem] * 8,
+        in_specs=[vmem] * 9,
         out_specs=vmem,
         scratch_shapes=[
             pltpu.VMEM((32, cells), BF16),
@@ -474,7 +503,9 @@
             pltpu.VMEM((32, cells), BF16),
             pltpu.VMEM((32, cells), BF16),
             pltpu.VMEM((192, 1728), BF16),
+            pltpu.VMEM((216, 576), BF16),
             pltpu.VMEM((n * per, blocks * PART), BF16),
+            pltpu.VMEM((blocks * PART, BY * LANES), BF16),
             pltpu.VMEM((2, blocks * PART, LANES), BF16),
             pltpu.VMEM((2, n * per, LANES), BF16),
             pltpu.SemaphoreType.DMA((2, 1)),
@@ -492,7 +523,7 @@
         cost_estimate=pl.CostEstimate(
             flops=1600000000, bytes_accessed=2000000, transcendentals=65536
         ),
-    )(flat, first, w_second, w_lift, third, w_affine, tissue, owners)
+    )(flat, rims, first, w_second, w_lift, w_merge, w_affine, tissue, owners)
     directions = w_affine.shape[0]
     routed = routed.reshape(2, n, SEND_CAP, PART // 2, 2, LANES)[:, :, :, :directions]
     routed = jnp.concatenate(

time: 39 us -> 35.4 us (0.908)
  Pallas kernels: 33.5 us -> 30.6 us
  local copies, waits for them, and re-layouts: 4.43 us -> 2.19 us
  matrix products: 0.49 us -> 2.05 us
    pallas_call x1, Pallas kernels: 33.5 us -> 30.6 us  [on_device(): pl.pallas_call(functools.partial(kernel, n, ny), out_shape=jax.ShapeDtype...]
    dot_general x1, matrix products: 0.49 us -> 2.05 us  [first_matrix(): jnp.einsum('oi,zik->zok', w_first, place, preferred_element_type=F32)]
    reshape x3 -> x0, local copies, waits for them, and re-layouts: 1.54 us -> none  [the longest x2 1.21 us: banded_weights(): w_merge.reshape(cu, 3, 3, 3, c1).transpose(3, 0, 2, 1, 4)]
    transpose x2 -> x0, local copies, waits for them, and re-layouts: 1.16 us -> none  [the longest x1 1.11 us: on_device(): flat = features.transpose(1, 0, 2, 3).reshape(depth * channels, cells)]
    another operation x1, local copies, waits for them, and re-layouts: 0.11 us -> 1.01 us  [on_device(): rims = jnp.stack([features[:, 0], features[:, depth - 1]])]
    unnamed x20 -> x18, local copies, waits for them, and re-layouts: 0.76 us -> 0.31 us
where the time goes in v3:
time: 35.4 us; the launch traced here: 35.2 us
  Pallas kernels  30.6 us (86%)
  local copies, waits for them, and re-layouts  2.19 us (6%)
  matrix products  2.05 us (6%)
    pallas_call x1, Pallas kernels, on_device(): pl.pallas_call(functools.partial(kernel, n, ny), out_shape=jax.ShapeDtype...  30.6 us
    dot_general x1, matrix products, first_matrix(): jnp.einsum('oi,zik->zok', w_first, place, preferred_element_type=F32)  2.05 us
    another operation x1, local copies, waits for them, and re-layouts, on_device(): rims = jnp.stack([features[:, 0], features[:, depth - 1]])  1.01 us

profile of v3, /device:TPU:0, one launch (start us, length us, event | category | flops | bytes accessed | tf_op | source)
XLA Modules:
  0.0 35.2 jit_solution(6277788708664805264)
XLA Ops:
  0.0 0.0 copy-start
  0.0 0.0 copy-start.7
  0.0 1.0 %slice_bitcast_fusion.1 = (bf16[1,12,32,128]{3,2,1,0:T(8,128)(2,1)S(1)}, bf16[1,12,32,128]{3,2,1,0:T(8,128)(2,1)S(1)}) fusion(bf16[12,4,32,128]{3,2,1,0:T(8,128)(2,1)} %param.9), kind=kLoop, calls=%fused_computation.9 | loop fusion | bytes 393216 | tf_op jit(solution)/shard_map/stack;squeeze | solution.py:485
  1.0 0.0 copy-start.1
  1.0 0.0 copy-start.2
  1.0 0.0 copy-start.3
  1.1 0.0 copy-start.4
  1.1 0.0 copy-start.5
  1.1 0.0 copy-start.6
  1.1 0.1 copy.28
  1.2 0.0 copy-done
  1.2 2.0 %convolution_convert_fusion = bf16[4,720,48]{1,2,0:T(8,128)(2,1)S(1)} fusion(bf16[4,324,720]{2,1,0:T(8,128)(2,1)} %constant.5.clone, bf16[48,324]{1,0:T(8,128)(2,1)S(1)} %copy-done), kind=kOutput, calls=%fused_computation | convolution fusion | flops 89717760 | bytes 2173824 | tf_op jit(solution)/shard_map/oi,zik->zok/dot_general | solution.py:475
  3.3 0.0 copy-done.7
  3.3 0.2 copy.27
  3.5 0.0 copy-done.1
  3.5 0.0 copy-done.2
  3.5 0.0 copy-done.3
  3.5 0.0 copy-done.4
  3.5 0.0 copy-done.5
  3.5 0.0 copy-done.6
  3.5 30.6 %shard_map.91 = bf16[2,16,16,128]{3,2,1,0:T(8,128)(2,1)S(1)} custom-call(bf16[48,4096]{1,0:T(8,128)(2,1)S(1)} %bitcast.30, bf16[32,4096]{1,0:T(8,128)(2,1)S(1)} %bitcast.32, bf16[192,720]{1,0:T(8,128)(2,1)S(1)} %bitcast.31, bf16[96,1296]{1,0:T(8,128)(2,1)S(1)} %copy-done.1, bf16[48,96]{1,0:T(8,128)(2,1)S(1)} %copy-done.3, bf16[12,1296]{1,0:T(8,128)(2,1)S(1)} %copy-done.2, ...), custom_call_target="tpu_custom_call" | custom-call | flops 1600000000 | bytes 2000000 | tf_op jit(solution)/shard_map/pallas_call | solution.py:491
  34.2 0.1 fusion.4
  34.4 0.2 pad_maximum_fusion
  34.5 0.7 %reshape.19 = bf16[1,16,2,1536]{3,2,1,0:T(2,128)(2,1)} reshape(bf16[16,2,3,4,128]{4,3,2,1,0:T(4,128)(2,1)S(1)} %pad_maximum_fusion) | data formatting | bytes 196608 | tf_op jit(solution)/shard_map/reshape | solution.py:532
  (5 shorter events, 0.1 us)
Async XLA Ops:
  0.0 1.2 %copy-start = (bf16[48,324]{1,0:T(8,128)(2,1)S(1)}, bf16[48,324]{1,0:T(8,128)(2,1)}, u32[]{:S(2)}) copy-start(bf16[48,324]{1,0:T(8,128)(2,1)} %param.10) | copy-start | bytes 93316
  0.0 3.3 %copy-start.7 = (bf16[12,4,32,128]{3,2,1,0:T(8,128)(2,1)S(1)}, bf16[12,4,32,128]{3,2,1,0:T(8,128)(2,1)}, u32[]{:S(2)}) copy-start(bf16[12,4,32,128]{3,2,1,0:T(8,128)(2,1)} %param.9) | copy-start | bytes 1179652
  1.0 2.5 %copy-start.1 = (bf16[96,1296]{1,0:T(8,128)(2,1)S(1)}, bf16[96,1296]{1,0:T(8,128)(2,1)}, u32[]{:S(2)}) copy-start(bf16[96,1296]{1,0:T(8,128)(2,1)} %w2_ref.1) | copy-start | bytes 746500
  1.0 2.5 %copy-start.2 = (bf16[12,1296]{1,0:T(8,128)(2,1)S(1)}, bf16[12,1296]{1,0:T(8,128)(2,1)}, u32[]{:S(2)}) copy-start(bf16[12,1296]{1,0:T(8,128)(2,1)} %w3_ref.1) | copy-start | bytes 93316
  1.0 2.5 %copy-start.3 = (bf16[48,96]{1,0:T(8,128)(2,1)S(1)}, bf16[48,96]{1,0:T(8,128)(2,1)}, u32[]{:S(2)}) copy-start(bf16[48,96]{1,0:T(8,128)(2,1)} %wl_ref.1) | copy-start | bytes 27652
  1.1 2.5 %copy-start.4 = (bf16[3,12]{1,0:T(4,128)(2,1)S(1)}, bf16[3,12]{1,0:T(4,128)(2,1)}, u32[]{:S(2)}) copy-start(bf16[3,12]{1,0:T(4,128)(2,1)} %wa_ref.1) | copy-start | bytes 220
  1.1 2.5 %copy-start.5 = (s32[1,32]{1,0:T(1,128)S(1)}, s32[1,32]{1,0:T(1,128)}, u32[]{:S(2)}) copy-start(s32[1,32]{1,0:T(1,128)} %tissue_ref.1) | copy-start | bytes 388
  1.1 2.4 %copy-start.6 = (s32[1,32]{1,0:T(1,128)S(1)}, s32[1,32]{1,0:T(1,128)}, u32[]{:S(2)}) copy-start(s32[1,32]{1,0:T(1,128)} %owners_ref.1) | copy-start | bytes 388

commit v4 on v3

--- a/solution.py
+++ b/solution.py
@@ -2,8 +2,6 @@
 
 import jax
 import jax.numpy as jnp
-import ml_dtypes
-import numpy as np
 from jax import lax
 from jax.experimental import pallas as pl
 from jax.experimental.pallas import tpu as pltpu
@@ -27,9 +25,9 @@
 
 def kernel(
     n, ny,
-    f_ref, rim_ref, w1_ref, w2_ref, wl_ref, w3_ref, wa_ref, tissue_ref, owners_ref,
+    f_ref, w1_ref, w2_ref, wl_ref, w3_ref, wa_ref, tissue_ref, owners_ref,
     out_ref,
-    fhalo, xpad, fmap, pool, mpad, terms, edge, ehalo, w2_band, w3_band, picks, masked, tiles, outgoing,
+    rim_ref, w1_band, carry, carry3, landing, fhalo, xpad, fmap, pool, mpad, terms, edge, ehalo, w2_band, w3_band, picks, masked, tiles, outgoing,
     fsend, frecv, psend, precv, esend, erecv, asend, arecv,
 ):
     me = lax.axis_index("gz")
@@ -108,6 +106,17 @@
                 go_right.wait_send()
 
         return start, receive, sent
+
+    f_rows = f_ref.shape[0]
+    depth = 4
+    rim_row = lax.broadcasted_iota(jnp.int32, (32, f_rows), 0)
+    rim_col = lax.broadcasted_iota(jnp.int32, (32, f_rows), 1)
+    rim_at = lax.rem(rim_row, 16) * depth + jnp.where(rim_row < 16, 0, depth - 1)
+    rim_pick = jnp.where(rim_at == rim_col, 1.0, 0.0).astype(BF16)
+    for at in range(0, cells, 1024):
+        rim_ref[:, at : at + 1024] = jnp.dot(
+            rim_pick, f_ref[:, at : at + 1024], preferred_element_type=F32
+        ).astype(BF16)
 
     pl.semaphore_wait(barrier, n - 1)
 
@@ -152,20 +161,43 @@
     w2_band[0:96, :] = jnp.concatenate([w2, blank], axis=1).astype(BF16)
     w2_band[96:192, :] = jnp.concatenate([blank, w2], axis=1).astype(BF16)
 
+    taps = w1_ref.shape[1]
+    tap = lax.broadcasted_iota(jnp.int32, (1, taps), 1)
+    w1 = w1_ref[...].astype(F32)
+    by_y = jnp.concatenate(
+        [jnp.where(lax.rem(tap // 36, 3) == b, w1, 0.0) for b in range(3)], axis=0
+    ).astype(BF16)
+    tap = lax.broadcasted_iota(jnp.int32, (taps, 1), 0)
+    channel = lax.rem(tap, 12)
+    x_off = lax.rem(tap // 12, 3)
+    z_off = tap // 108
+    target = lax.broadcasted_iota(jnp.int32, (taps, 240), 1)
+    for z in range(depth):
+        plane = z_off + (z - 1)
+        row = jnp.where(
+            plane < 0,
+            channel,
+            jnp.where(plane == depth, 64 + channel, 16 + depth * channel + plane),
+        )
+        place = jnp.where(target == x_off * 80 + row, 1.0, 0.0).astype(BF16)
+        w1_band[144 * z : 144 * z + 144, :] = jnp.dot(
+            by_y, place, preferred_element_type=F32
+        ).astype(BF16)
+
     w3 = w3_ref[...].astype(F32)
     bands = []
-    for c_off in range(3):
+    for bc in range(9):
         columns = jnp.concatenate(
-            [w3[:, (3 * ab + c_off) * 48 : (3 * ab + c_off) * 48 + 48] for ab in range(9)], axis=1
+            [w3[:, (9 * a + bc) * 48 : (9 * a + bc) * 48 + 48] for a in range(3)], axis=1
         )
         for zo in range(6):
-            first = 144 * (zo - 2)
-            low, high = max(first, 0), min(first + 432, 576)
+            first = 48 * (zo - 2)
+            low, high = max(first, 0), min(first + 144, 192)
             pieces = [columns[:, low - first : high - first]]
             if low > 0:
                 pieces.insert(0, jnp.zeros((12, low), F32))
-            if high < 576:
-                pieces.append(jnp.zeros((12, 576 - high), F32))
+            if high < 192:
+                pieces.append(jnp.zeros((12, 192 - high), F32))
             bands.append(jnp.concatenate(pieces, axis=1))
     w3_band[...] = jnp.concatenate(bands, axis=0).astype(BF16)
 
@@ -200,16 +232,33 @@
         pool[row0 : row0 + rows, to] = lane_shift(v, 2, lane).astype(BF16)
         pool[384 + row0 : 384 + row0 + rows, to] = lane_shift(v, -2, lane).astype(BF16)
 
+    def sum_rows(product, offset, held):
+        one = slice(0, LANES)
+        two = slice(LANES, 2 * LANES)
+        done = [
+            held[0] + offset(product, 2, one),
+            held[1] + offset(product, 1, one) + offset(product, 2, two),
+        ]
+        held[0] = offset(product, 0, one) + offset(product, 1, two)
+        held[1] = offset(product, 0, two)
+        return done
+
+    def first_offset(product, b, at):
+        return jnp.concatenate(
+            [product[144 * z + 48 * b : 144 * z + 48 * b + 48, at] for z in range(depth)], axis=0
+        )
+
+    def first_product(pair):
+        at = pl.ds(pl.multiple_of(pair * 2 * LANES, 2 * LANES), 2 * LANES)
+        return jnp.dot(w1_band[...], xpad[:, at], preferred_element_type=F32)
+
+    carry[...] = jnp.zeros(carry.shape, F32)
+    sum_rows(first_product(0), first_offset, carry)
+
     def first_conv(i, _):
         base = pl.multiple_of(i * 2 * LANES, 2 * LANES)
-        patch = jnp.concatenate(
-            [
-                xpad[:, pl.ds(pl.multiple_of(base + b * LANES, LANES), 2 * LANES)]
-                for b in range(3)
-            ],
-            axis=0,
-        )
-        acc = jnp.maximum(jnp.dot(w1_ref[...], patch, preferred_element_type=F32), 0.0)
+        acc = jnp.concatenate(sum_rows(first_product(i + 1), first_offset, carry), axis=1)
+        acc = jnp.maximum(acc, 0.0)
         fmap[:, pl.ds(base, 2 * LANES)] = acc.astype(BF16)
         deep = jnp.concatenate(
             [jnp.maximum(acc[0:48], acc[48:96]), jnp.maximum(acc[96:144], acc[144:192])], axis=0
@@ -291,27 +340,24 @@
         last = (seg + 1) * per_seg - (0 if seg == SEGS - 1 else 1)
         lax.fori_loop(first, last, second_conv, 0, unroll=True)
 
+    def third_offset(product, b, at):
+        return product[216 * b : 216 * b + 216, at]
+
+    def third_product(pair):
+        at = pl.ds(pl.multiple_of(pair * 2 * LANES, 2 * LANES), 2 * LANES)
+        return jnp.dot(w3_band[...], mpad[:, at], preferred_element_type=F32)
+
+    carry3[...] = jnp.zeros(carry3.shape, F32)
+    sum_rows(third_product(0), third_offset, carry3)
+
     def third_conv(i, _):
         base = pl.multiple_of(i * 2 * LANES, 2 * LANES)
-        patch = jnp.concatenate(
-            [
-                mpad[
-                    48 * plane : 48 * plane + 48,
-                    pl.ds(pl.multiple_of(base + b * LANES, LANES), 2 * LANES),
-                ]
-                for plane in range(4)
-                for b in range(3)
-            ],
-            axis=0,
-        )
-        acc = jnp.dot(w3_band[...], patch, preferred_element_type=F32)
+        done = sum_rows(third_product(i + 1), third_offset, carry3)
         lane = lanes_of(72)
         for row in range(2):
-            at = slice(row * LANES, (row + 1) * LANES)
+            acc = done[row]
             total = (
-                acc[72:144, at]
-                + lane_shift(acc[0:72, at], 1, lane)
-                + lane_shift(acc[144:216, at], -1, lane)
+                acc[72:144] + lane_shift(acc[0:72], 1, lane) + lane_shift(acc[144:216], -1, lane)
             )
             to = pl.ds(pl.multiple_of(base + row * LANES, LANES), LANES)
             terms[:, to] = total
@@ -396,7 +442,7 @@
         target = lax.rem(me + step, n)
         return remote(
             outgoing.at[part, pl.ds(pl.multiple_of(target * per, per), per)],
-            out_ref.at[part, me], asend.at[part, step], arecv.at[part, step], target,
+            landing.at[part, me], asend.at[part, step], arecv.at[part, step], target,
         )
 
     def send_part(part):
@@ -415,7 +461,7 @@
 
         lax.fori_loop(0, groups, route, 0)
         lax.fori_loop(1, n, send, 0)
-        out_ref[part, me] = outgoing[part, pl.ds(pl.multiple_of(me * per, per), per), :]
+        landing[part, me] = outgoing[part, pl.ds(pl.multiple_of(me * per, per), per), :]
 
     inner_head = head_rows(head_matrix(24, 0, 12), lambda at: terms[24:48, at])
     lax.fori_loop(0, ny // BY, inner_head, 0, unroll=2)
@@ -455,25 +501,27 @@
 
     lax.fori_loop(1, n, receive, 0)
 
-
-def first_matrix(w_first, depth):
-    c1, c0 = w_first.shape[0], w_first.shape[1] // 27
-    place = np.zeros((depth, 3, 9, c0, 9, 80), np.float32)
-    for z in range(depth):
-        for a in range(3):
-            for i in range(c0):
-                plane = z + a - 1
-                if plane < 0:
-                    row = i
-                elif plane == depth:
-                    row = 64 + i
-                else:
-                    row = 16 + depth * i + plane
-                for bc in range(9):
-                    place[z, a, bc, i, bc, row] = 1
-    place = place.reshape(depth, 27 * c0, 720).astype(ml_dtypes.bfloat16)
-    first = jnp.einsum("oi,zik->zok", w_first, place, preferred_element_type=F32)
-    return first.astype(BF16).reshape(depth * c1, 720)
+    slots = n * SEND_CAP
+    used = 2 * directions
+    line = lax.broadcasted_iota(jnp.int32, (used * slots, slots * PART), 0)
+    source = lax.rem(line, slots) * PART + line // slots
+    gather = jnp.where(
+        source == lax.broadcasted_iota(jnp.int32, (used * slots, slots * PART), 1), 1.0, 0.0
+    ).astype(BF16)
+    inner_rows, outer_rows = [
+        jnp.dot(
+            gather, landing[part].reshape(slots * PART, LANES), preferred_element_type=F32
+        )
+        for part in range(2)
+    ]
+    lines = []
+    for d in range(directions):
+        for rows_of, turn in ((outer_rows, 0), (inner_rows, 0), (inner_rows, 1), (outer_rows, 1)):
+            k = (2 * d + turn) * slots
+            lines.append(rows_of[k : k + slots])
+    whole = jnp.concatenate(lines, axis=1)
+    for s in range(n):
+        out_ref[s] = whole[SEND_CAP * s : SEND_CAP * s + SEND_CAP].astype(BF16)
 
 
 def on_device(features, w_first, w_second, w_lift, w_merge, w_affine, tissue, owners):
@@ -482,18 +530,20 @@
     cells = ny * nx
     hcells = (ny // 2) * nx
     flat = features.reshape(channels * depth, cells)
-    rims = jnp.stack([features[:, 0], features[:, depth - 1]])
-    rims = jnp.pad(rims, ((0, 0), (0, 16 - channels), (0, 0), (0, 0))).reshape(32, cells)
-    first = first_matrix(w_first, depth)
     per = SEND_CAP * PART
     blocks = (ny // BY) * (nx // BX)
     vmem = pl.BlockSpec(memory_space=pltpu.VMEM)
     routed = pl.pallas_call(
         functools.partial(kernel, n, ny),
-        out_shape=jax.ShapeDtypeStruct((2, n, per, LANES), BF16),
-        in_specs=[vmem] * 9,
+        out_shape=jax.ShapeDtypeStruct((n, SEND_CAP, w_affine.shape[0] * depth * LANES), BF16),
+        in_specs=[vmem] * 8,
         out_specs=vmem,
         scratch_shapes=[
+            pltpu.VMEM((32, cells), BF16),
+            pltpu.VMEM((576, 240), BF16),
+            pltpu.VMEM((2, 192, LANES), F32),
+            pltpu.VMEM((2, 216, LANES), F32),
+            pltpu.VMEM((2, n, per, LANES), BF16),
             pltpu.VMEM((32, cells), BF16),
             pltpu.VMEM((240, cells + 2 * LANES), BF16),
             pltpu.VMEM((192, cells), BF16),
@@ -503,7 +553,7 @@
             pltpu.VMEM((32, cells), BF16),
             pltpu.VMEM((32, cells), BF16),
             pltpu.VMEM((192, 1728), BF16),
-            pltpu.VMEM((216, 576), BF16),
+            pltpu.VMEM((648, 192), BF16),
             pltpu.VMEM((n * per, blocks * PART), BF16),
             pltpu.VMEM((blocks * PART, BY * LANES), BF16),
             pltpu.VMEM((2, blocks * PART, LANES), BF16),
@@ -523,13 +573,8 @@
         cost_estimate=pl.CostEstimate(
             flops=1600000000, bytes_accessed=2000000, transcendentals=65536
         ),
-    )(flat, rims, first, w_second, w_lift, w_merge, w_affine, tissue, owners)
-    directions = w_affine.shape[0]
-    routed = routed.reshape(2, n, SEND_CAP, PART // 2, 2, LANES)[:, :, :, :directions]
-    routed = jnp.concatenate(
-        [routed[1, :, :, :, :1], routed[0], routed[1, :, :, :, 1:]], axis=3
-    )
-    return routed.reshape(1, n, SEND_CAP, directions * depth * LANES)
+    )(flat, w_first, w_second, w_lift, w_merge, w_affine, tissue, owners)
+    return routed[None]
 
 
 def solution(mesh):

time: 35.4 us -> 33.7 us (0.952)
  matrix products: 2.05 us -> 0 us
  Pallas kernels: 30.6 us -> 31 us
    unnamed x18 -> x16, local copies, waits for them, and re-layouts: 0.31 us -> 2.47 us
    dot_general x1 -> x0, matrix products: 2.05 us -> none  [first_matrix(): jnp.einsum('oi,zik->zok', w_first, place, preferred_element_type=F32)]
    another operation x1 -> x0, local copies, waits for them, and re-layouts: 1.01 us -> none  [on_device(): rims = jnp.stack([features[:, 0], features[:, depth - 1]])]
    reshape x1 -> x0, local copies, waits for them, and re-layouts: 0.67 us -> none  [on_device(): return routed.reshape(1, n, SEND_CAP, directions * depth * LANES)]
    pallas_call x1, Pallas kernels: 30.6 us -> 31 us  [on_device(): pl.pallas_call(functools.partial(kernel, n, ny), out_shape=jax.ShapeDtype...]
where the time goes in v4:
time: 33.7 us; the launch traced here: 33.5 us
  Pallas kernels  31 us (92%)
  local copies, waits for them, and re-layouts  2.47 us (7%)
    pallas_call x1, Pallas kernels, on_device(): pl.pallas_call(functools.partial(kernel, n, ny), out_shape=jax.ShapeDtype...  31 us
    unnamed x16, local copies, waits for them, and re-layouts  2.47 us

profile of v4, /device:TPU:0, one launch (start us, length us, event | category | flops | bytes accessed | tf_op | source)
XLA Modules:
  0.0 33.5 jit_solution(8436997826181673493)
XLA Ops:
  0.0 0.0 copy-start
  0.0 0.0 copy-start.1
  0.0 0.0 copy-start.2
  0.0 0.0 copy-start.3
  0.0 0.0 copy-start.6
  0.0 1.2 %copy.11 = bf16[6,8,32,128]{3,1,2,0:T(8,128)(2,1)S(1)} copy(bf16[6,8,32,128]{3,2,1,0:T(8,128)(2,1)} %bitcast.8) | data formatting | bytes 786432
  1.2 0.0 copy-start.4
  1.2 0.0 copy-start.5
  1.2 0.0 copy-done
  1.2 0.0 copy-done.1
  1.3 0.0 copy-done.2
  1.3 0.0 copy-done.3
  1.3 0.0 copy-done.6
  1.3 0.6 %copy-done.4 = bf16[3,12]{1,0:T(4,128)(2,1)S(1)} copy-done((bf16[3,12]{1,0:T(4,128)(2,1)S(1)}, bf16[3,12]{1,0:T(4,128)(2,1)}, u32[]{:S(2)}) %copy-start.4) | copy-done | bytes 96
  1.9 0.0 copy-done.5
  1.9 31.0 %shard_map.82 = bf16[16,2,1536]{2,1,0:T(2,128)(2,1)S(1)} custom-call(bf16[48,4096]{1,0:T(8,128)(2,1)S(1)} %bitcast.6, bf16[48,324]{1,0:T(8,128)(2,1)S(1)} %copy-done.2, bf16[96,1296]{1,0:T(8,128)(2,1)S(1)} %copy-done, bf16[48,96]{1,0:T(8,128)(2,1)S(1)} %copy-done.3, bf16[12,1296]{1,0:T(8,128)(2,1)S(1)} %copy-done.1, bf16[3,12]{1,0:T(4,128)(2,1)S(1)} %copy-done.4, ...), custom_call_target="tpu_custom_call" | custom-call | flops 1600000000 | bytes 2000000 | tf_op jit(solution)/shard_map/pallas_call | solution.py:536
  32.9 0.6 %copy.13 = bf16[1,16,2,1536]{3,2,1,0:T(2,128)(2,1)} copy(bf16[1,16,2,1536]{3,2,1,0:T(2,128)(2,1)S(1)} %bitcast.7) | data formatting | bytes 196608
Async XLA Ops:
  0.0 1.2 %copy-start = (bf16[96,1296]{1,0:T(8,128)(2,1)S(1)}, bf16[96,1296]{1,0:T(8,128)(2,1)}, u32[]{:S(2)}) copy-start(bf16[96,1296]{1,0:T(8,128)(2,1)} %w2_ref.1) | copy-start | bytes 746500
  0.0 1.2 %copy-start.1 = (bf16[12,1296]{1,0:T(8,128)(2,1)S(1)}, bf16[12,1296]{1,0:T(8,128)(2,1)}, u32[]{:S(2)}) copy-start(bf16[12,1296]{1,0:T(8,128)(2,1)} %w3_ref.1) | copy-start | bytes 93316
  0.0 1.3 %copy-start.2 = (bf16[48,324]{1,0:T(8,128)(2,1)S(1)}, bf16[48,324]{1,0:T(8,128)(2,1)}, u32[]{:S(2)}) copy-start(bf16[48,324]{1,0:T(8,128)(2,1)} %w1_ref.1) | copy-start | bytes 93316
  0.0 1.3 %copy-start.3 = (bf16[48,96]{1,0:T(8,128)(2,1)S(1)}, bf16[48,96]{1,0:T(8,128)(2,1)}, u32[]{:S(2)}) copy-start(bf16[48,96]{1,0:T(8,128)(2,1)} %wl_ref.1) | copy-start | bytes 27652
  0.0 1.3 %copy-start.6 = (s32[1,32]{1,0:T(1,128)S(1)}, s32[1,32]{1,0:T(1,128)}, u32[]{:S(2)}) copy-start(s32[1,32]{1,0:T(1,128)} %owners_ref.1) | copy-start | bytes 388
  1.2 0.7 %copy-start.4 = (bf16[3,12]{1,0:T(4,128)(2,1)S(1)}, bf16[3,12]{1,0:T(4,128)(2,1)}, u32[]{:S(2)}) copy-start(bf16[3,12]{1,0:T(4,128)(2,1)} %wa_ref.1) | copy-start | bytes 220
  1.2 0.7 %copy-start.5 = (s32[1,32]{1,0:T(1,128)S(1)}, s32[1,32]{1,0:T(1,128)}, u32[]{:S(2)}) copy-start(s32[1,32]{1,0:T(1,128)} %tissue_ref.1) | copy-start | bytes 388

commit v5 on v4

--- a/solution.py
+++ b/solution.py
@@ -25,8 +25,9 @@
 
 def kernel(
     n, ny,
-    f_ref, w1_ref, w2_ref, wl_ref, w3_ref, wa_ref, tissue_ref, owners_ref,
+    f_in, w1_in, w2_in, wl_in, w3_in, wa_in, tissue_in, owners_in,
     out_ref,
+    f_ref, w1_ref, w2_ref, wl_ref, w3_ref, wa_ref, tissue_ref, owners_ref, own_sem, planes,
     rim_ref, w1_band, carry, carry3, landing, fhalo, xpad, fmap, pool, mpad, terms, edge, ehalo, w2_band, w3_band, picks, masked, tiles, outgoing,
     fsend, frecv, psend, precv, esend, erecv, asend, arecv,
 ):
@@ -39,6 +40,15 @@
     hy = ny // 2
     hcells = hy * LANES
 
+    sources = (f_in, w1_in, w2_in, wl_in, w3_in, wa_in, tissue_in, owners_in)
+    held_here = (f_ref, w1_ref, w2_ref, wl_ref, w3_ref, wa_ref, tissue_ref, owners_ref)
+    loads = [
+        pltpu.make_async_copy(source, place, own_sem.at[k])
+        for k, (source, place) in enumerate(zip(sources, held_here))
+    ]
+    for load in loads:
+        load.start()
+
     barrier = pltpu.get_barrier_semaphore()
 
     def greet(step, _):
@@ -107,16 +117,19 @@
 
         return start, receive, sent
 
+    depth = 4
     f_rows = f_ref.shape[0]
-    depth = 4
-    rim_row = lax.broadcasted_iota(jnp.int32, (32, f_rows), 0)
-    rim_col = lax.broadcasted_iota(jnp.int32, (32, f_rows), 1)
-    rim_at = lax.rem(rim_row, 16) * depth + jnp.where(rim_row < 16, 0, depth - 1)
-    rim_pick = jnp.where(rim_at == rim_col, 1.0, 0.0).astype(BF16)
-    for at in range(0, cells, 1024):
-        rim_ref[:, at : at + 1024] = jnp.dot(
-            rim_pick, f_ref[:, at : at + 1024], preferred_element_type=F32
-        ).astype(BF16)
+    channels_in = f_rows // depth
+    loads[0].wait()
+    planes[...] = f_ref[...].reshape(f_rows * ny, LANES).astype(F32)
+    rim_pad = jnp.zeros((16 - channels_in, LANES), F32)
+    for y in range(ny):
+        at = slice(y * LANES, (y + 1) * LANES)
+        for side in range(2):
+            rim = planes[pl.ds(side * (depth - 1) * ny + y, channels_in, stride=depth * ny), :]
+            rim_ref[16 * side : 16 * side + 16, at] = jnp.concatenate(
+                [rim, rim_pad], axis=0
+            ).astype(BF16)
 
     pl.semaphore_wait(barrier, n - 1)
 
@@ -124,6 +137,8 @@
         rim_ref.at[0:16], fhalo.at[16:32], rim_ref.at[16:32], fhalo.at[0:16], fsend, frecv, 0
     )
     features_start()
+    for load in loads[1:]:
+        load.wait()
 
     nbx = LANES // BX
     count = tissue_ref.shape[1]
@@ -201,28 +216,24 @@
             bands.append(jnp.concatenate(pieces, axis=1))
     w3_band[...] = jnp.concatenate(bands, axis=0).astype(BF16)
 
-    def shift_rows(v, row0, to):
-        rows = v.shape[0]
+    def shift_rows(vf, row0, to):
+        rows = vf.shape[0]
         lane = lanes_of(rows)
-        vf = v.astype(F32)
         xpad[row0 : row0 + rows, to] = lane_shift(vf, 1, lane).astype(BF16)
-        xpad[80 + row0 : 80 + row0 + rows, to] = v
+        xpad[80 + row0 : 80 + row0 + rows, to] = vf.astype(BF16)
         xpad[160 + row0 : 160 + row0 + rows, to] = lane_shift(vf, -1, lane).astype(BF16)
 
-    def shift_own(y, _):
-        at = pl.ds(pl.multiple_of(y * LANES, LANES), LANES)
-        to = pl.ds(pl.multiple_of((y + 1) * LANES, LANES), LANES)
-        shift_rows(f_ref[:, at], 16, to)
-        return 0
-
-    lax.fori_loop(0, ny, shift_own, 0, unroll=4)
+    for y in range(ny):
+        shift_rows(
+            planes[pl.ds(y, f_rows, stride=ny), :], 16, slice((y + 1) * LANES, (y + 2) * LANES)
+        )
     features_receive()
 
     def shift_rims(y, _):
         at = pl.ds(pl.multiple_of(y * LANES, LANES), LANES)
         to = pl.ds(pl.multiple_of((y + 1) * LANES, LANES), LANES)
-        shift_rows(fhalo[0:16, at], 0, to)
-        shift_rows(fhalo[16:32, at], 64, to)
+        shift_rows(fhalo[0:16, at].astype(F32), 0, to)
+        shift_rows(fhalo[16:32, at].astype(F32), 64, to)
         return 0
 
     lax.fori_loop(0, ny, shift_rims, 0, unroll=4)
@@ -529,16 +540,20 @@
     channels, depth, ny, nx = features.shape
     cells = ny * nx
     hcells = (ny // 2) * nx
-    flat = features.reshape(channels * depth, cells)
+    flat = features.reshape(channels * depth, ny, nx)
+    operands = (flat, w_first, w_second, w_lift, w_merge, w_affine, tissue, owners)
     per = SEND_CAP * PART
     blocks = (ny // BY) * (nx // BX)
     vmem = pl.BlockSpec(memory_space=pltpu.VMEM)
     routed = pl.pallas_call(
         functools.partial(kernel, n, ny),
         out_shape=jax.ShapeDtypeStruct((n, SEND_CAP, w_affine.shape[0] * depth * LANES), BF16),
-        in_specs=[vmem] * 8,
+        in_specs=[pl.BlockSpec(memory_space=pltpu.HBM)] * len(operands),
         out_specs=vmem,
         scratch_shapes=[
+            *[pltpu.VMEM(operand.shape, operand.dtype) for operand in operands],
+            pltpu.SemaphoreType.DMA((len(operands),)),
+            pltpu.VMEM((channels * depth * ny, LANES), F32),
             pltpu.VMEM((32, cells), BF16),
             pltpu.VMEM((576, 240), BF16),
             pltpu.VMEM((2, 192, LANES), F32),
@@ -568,12 +583,12 @@
             pltpu.SemaphoreType.DMA((2, n)),
         ],
         compiler_params=pltpu.CompilerParams(
-            collective_id=0, has_side_effects=True, vmem_limit_bytes=48 * 1024 * 1024
+            collective_id=0, has_side_effects=True, vmem_limit_bytes=63 * 1024 * 1024
         ),
         cost_estimate=pl.CostEstimate(
             flops=1600000000, bytes_accessed=2000000, transcendentals=65536
         ),
-    )(flat, w_first, w_second, w_lift, w_merge, w_affine, tissue, owners)
+    )(*operands)
     return routed[None]
 
 

time: 33.7 us -> 33.5 us (level)
  local copies, waits for them, and re-layouts: 2.47 us -> 1.6 us
  Pallas kernels: 31 us -> 31.7 us
    unnamed x16 -> x1, local copies, waits for them, and re-layouts: 2.47 us -> 1.6 us
    pallas_call x1, Pallas kernels: 31 us -> 31.7 us  [on_device(): pl.pallas_call(functools.partial(kernel, n, ny), out_shape=jax.ShapeDtype...]
where the time goes in v5:
time: 33.5 us; the launch traced here: 33.4 us
  Pallas kernels  31.7 us (95%)
  local copies, waits for them, and re-layouts  1.6 us (5%)
    pallas_call x1, Pallas kernels, on_device(): pl.pallas_call(functools.partial(kernel, n, ny), out_shape=jax.ShapeDtype...  31.7 us
    unnamed x1, local copies, waits for them, and re-layouts  1.6 us

profile of v5, /device:TPU:0, one launch (start us, length us, event | category | flops | bytes accessed | tf_op | source)
XLA Modules:
  0.0 33.4 jit_solution(15639829877127730683)
XLA Ops:
  0.0 31.7 %shard_map.82 = bf16[16,2,1536]{2,1,0:T(2,128)(2,1)} custom-call(bf16[48,32,128]{2,1,0:T(8,128)(2,1)} %bitcast.3, bf16[48,324]{1,0:T(8,128)(2,1)} %w1_in.1, bf16[96,1296]{1,0:T(8,128)(2,1)} %w2_in.1, bf16[48,96]{1,0:T(8,128)(2,1)} %wl_in.1, bf16[12,1296]{1,0:T(8,128)(2,1)} %w3_in.1, bf16[3,12]{1,0:T(4,128)(2,1)} %wa_in.1, s32[1,32]{1,0:T(1,128)} %tissue_in.1, ...), custom_call_target="tpu_custom_call" | custom-call | flops 1600000000 | bytes 2000000 | tf_op jit(solution)/shard_map/pallas_call | solution.py:548
  31.8 1.6 %copy.10 = bf16[1,16,2,1536]{3,2,1,0:T(2,128)(2,1)} copy(bf16[1,16,2,1536]{3,2,1,0:T(2,128)(2,1)} %bitcast.2) | data formatting | bytes 196608

commit v6 on v5

--- a/solution.py
+++ b/solution.py
@@ -28,7 +28,7 @@
     f_in, w1_in, w2_in, wl_in, w3_in, wa_in, tissue_in, owners_in,
     out_ref,
     f_ref, w1_ref, w2_ref, wl_ref, w3_ref, wa_ref, tissue_ref, owners_ref, own_sem, planes,
-    rim_ref, w1_band, carry, carry3, landing, fhalo, xpad, fmap, pool, mpad, terms, edge, ehalo, w2_band, w3_band, picks, masked, tiles, outgoing,
+    rim_ref, w1_band, carry, carry3, landing, fhalo, xpad, fmap, rows_max, pool, shares, mpad, terms, edge, ehalo, w2_band, w3_band, picks, masked, tiles, outgoing,
     fsend, frecv, psend, precv, esend, erecv, asend, arecv,
 ):
     me = lax.axis_index("gz")
@@ -65,8 +65,9 @@
 
     xpad[:, 0:LANES] = jnp.zeros((240, LANES), BF16)
     xpad[:, cells + LANES : cells + 2 * LANES] = jnp.zeros((240, LANES), BF16)
-    pool[:, 0:LANES] = jnp.zeros((576, LANES), BF16)
-    pool[:, hcells + LANES : hcells + 2 * LANES] = jnp.zeros((576, LANES), BF16)
+    border = jnp.zeros((576, LANES), F32)
+    shares[:, 0:LANES] = border
+    shares[:, hcells // 2 + LANES : hcells // 2 + 2 * LANES] = border
     mpad[:, 0:LANES] = jnp.zeros((192, LANES), BF16)
     mpad[:, cells + LANES : cells + 2 * LANES] = jnp.zeros((192, LANES), BF16)
 
@@ -172,9 +173,13 @@
     lax.fori_loop(0, groups, pick_rows, 0)
 
     w2 = w2_ref[...].astype(F32)
-    blank = jnp.zeros((96, 432), F32)
-    w2_band[0:96, :] = jnp.concatenate([w2, blank], axis=1).astype(BF16)
-    w2_band[96:192, :] = jnp.concatenate([blank, w2], axis=1).astype(BF16)
+    blank = jnp.zeros((96, 144), F32)
+    for b in range(3):
+        taps = [w2[:, 432 * a + 144 * b : 432 * a + 144 * b + 144] for a in range(3)]
+        for z in range(2):
+            w2_band[192 * b + 96 * z : 192 * b + 96 * z + 96, :] = jnp.concatenate(
+                [blank] * z + taps + [blank] * (1 - z), axis=1
+            ).astype(BF16)
 
     taps = w1_ref.shape[1]
     tap = lax.broadcasted_iota(jnp.int32, (1, taps), 1)
@@ -238,10 +243,14 @@
 
     lax.fori_loop(0, ny, shift_rims, 0, unroll=4)
 
-    def shift_pool(row0, rows, v, to):
-        lane = lanes_of(rows)
-        pool[row0 : row0 + rows, to] = lane_shift(v, 2, lane).astype(BF16)
-        pool[384 + row0 : 384 + row0 + rows, to] = lane_shift(v, -2, lane).astype(BF16)
+    half = LANES // 2
+
+    def shift_pool(plane, v, to):
+        at = lax.rem(lanes_of(48), half)
+        before = jnp.where(at >= 1, pltpu.roll(v, 1, axis=1), 0.0)
+        after = jnp.where(at < half - 1, pltpu.roll(v, LANES - 1, axis=1), 0.0)
+        pool[144 * plane : 144 * plane + 48, to] = before.astype(BF16)
+        pool[144 * plane + 96 : 144 * plane + 144, to] = after.astype(BF16)
 
     def sum_rows(product, offset, held):
         one = slice(0, LANES)
@@ -275,81 +284,100 @@
             [jnp.maximum(acc[0:48], acc[48:96]), jnp.maximum(acc[96:144], acc[144:192])], axis=0
         )
         wide = jnp.maximum(deep[:, 0:LANES], deep[:, LANES : 2 * LANES])
-        even = lax.rem(lanes_of(96), 2) == 0
-        other = jnp.where(
-            even, pltpu.roll(wide, LANES - 1, axis=1), pltpu.roll(wide, 1, axis=1)
-        )
-        both = jnp.maximum(wide, other)
-        to = pl.ds(pl.multiple_of((i + 1) * LANES, LANES), LANES)
-        pool[240:336, to] = both.astype(BF16)
-        shift_pool(48, 96, both, to)
-        return 0
+        both = jnp.maximum(wide, pltpu.roll(wide, LANES - 1, axis=1))
+        rows_max[:, pl.ds(pl.multiple_of(i * LANES, LANES), LANES)] = both.astype(BF16)
+        return 0
+
+    compact = jnp.where(
+        lax.broadcasted_iota(jnp.int32, (2 * LANES, LANES), 0)
+        == 2 * lax.broadcasted_iota(jnp.int32, (2 * LANES, LANES), 1),
+        1.0,
+        0.0,
+    ).astype(BF16)
+    double = jnp.where(
+        lax.broadcasted_iota(jnp.int32, (LANES, 2 * LANES), 0)
+        == lax.broadcasted_iota(jnp.int32, (LANES, 2 * LANES), 1) // 2,
+        1.0,
+        0.0,
+    ).astype(BF16)
 
     seg_rows = hy // SEGS
 
     def pooled(seg):
-        at = pl.ds(pl.multiple_of((seg * seg_rows + 1) * LANES, LANES), seg_rows * LANES)
+        at = pl.ds(pl.multiple_of(seg * 2 * LANES, 2 * LANES), 2 * LANES)
         return exchange(
-            pool.at[240:288, at], pool.at[336:384, at],
-            pool.at[288:336, at], pool.at[192:240, at], psend, precv, seg,
-        )
+            pool.at[192:240, at], pool.at[480:528, at],
+            pool.at[336:384, at], pool.at[48:96, at], psend, precv, seg,
+        )
+
+    def tile_at(tile):
+        return pl.ds(pl.multiple_of(tile * LANES, LANES), LANES)
 
     def first_segment(seg, _):
         lax.fori_loop(
             0, seg_rows, lambda i, _: first_conv(seg * seg_rows + i, 0), 0, unroll=True
         )
+        pairs = [
+            rows_max[:, pl.ds(pl.multiple_of((2 * seg + t) * 2 * LANES, 2 * LANES), 2 * LANES)]
+            for t in range(2)
+        ]
+        packed = jnp.dot(jnp.concatenate(pairs, axis=0), compact, preferred_element_type=F32)
+        for t in range(2):
+            for z in range(2):
+                pool[144 * z + 192 : 144 * z + 240, tile_at(2 * seg + t)] = packed[
+                    96 * t + 48 * z : 96 * t + 48 * z + 48
+                ].astype(BF16)
         pooled(seg)[0]()
+        for t in range(2):
+            for z in range(2):
+                shift_pool(
+                    z + 1, packed[96 * t + 48 * z : 96 * t + 48 * z + 48], tile_at(2 * seg + t)
+                )
         return 0
 
     lax.fori_loop(0, SEGS, first_segment, 0)
 
-    def shift_halo(y, _):
-        to = pl.ds(pl.multiple_of((y + 1) * LANES, LANES), LANES)
-        shift_pool(0, 48, pool[192:240, to].astype(F32), to)
-        shift_pool(144, 48, pool[336:384, to].astype(F32), to)
-        return 0
+    def second_segment(seg, _):
+        pooled(seg)[1]()
+        for t in range(2):
+            to = tile_at(2 * seg + t)
+            shift_pool(0, pool[48:96, to].astype(F32), to)
+            shift_pool(3, pool[480:528, to].astype(F32), to)
+        at = pl.ds(pl.multiple_of(seg * 2 * LANES, 2 * LANES), 2 * LANES)
+        to = pl.ds(pl.multiple_of((2 * seg + 1) * LANES, LANES), 2 * LANES)
+        shares[:, to] = jnp.dot(w2_band[...], pool[:, at], preferred_element_type=F32)
+        return 0
+
+    lax.fori_loop(0, SEGS, second_segment, 0)
 
     def second_conv(i, _):
-        base = pl.multiple_of(i * 2 * LANES, 2 * LANES)
-        patch = jnp.concatenate(
-            [
-                pool[
-                    192 * c + 48 * plane : 192 * c + 48 * plane + 48,
-                    pl.ds(pl.multiple_of(base + b * LANES, LANES), 2 * LANES),
-                ]
-                for plane in range(4)
-                for b in range(3)
-                for c in range(3)
-            ],
-            axis=0,
-        )
-        acc = jnp.dot(w2_band[...], patch, preferred_element_type=F32)
+        lower = lanes_of(192) < half
+
+        def turned(row0, tile):
+            return pltpu.roll(shares[row0 : row0 + 192, tile_at(tile)], half, axis=1)
+
+        acc = (
+            shares[192:384, tile_at(i + 1)]
+            + jnp.where(lower, turned(0, i), turned(0, i + 1))
+            + jnp.where(lower, turned(384, i + 1), turned(384, i + 2))
+        )
         second = jnp.maximum(acc, 0.0).astype(BF16)
-        for half in range(2):
+        second = jnp.dot(second, double, preferred_element_type=F32).astype(BF16)
+        for side in range(2):
             lifted = jnp.dot(
-                wl_ref[...], second[96 * half : 96 * half + 96], preferred_element_type=F32
+                wl_ref[...], second[96 * side : 96 * side + 96], preferred_element_type=F32
             )
             for row in range(4):
                 part = lifted[:, (row // 2) * LANES : (row // 2 + 1) * LANES]
                 for deep in range(2):
-                    plane = 48 * (2 * half + deep)
-                    own = fmap[
-                        plane : plane + 48,
-                        pl.ds(pl.multiple_of(i * 4 * LANES + row * LANES, LANES), LANES),
-                    ]
-                    mpad[
-                        plane : plane + 48,
-                        pl.ds(pl.multiple_of(i * 4 * LANES + (row + 1) * LANES, LANES), LANES),
-                    ] = (part + own.astype(F32)).astype(BF16)
-        return 0
-
-    per_seg = seg_rows // 2
-    for seg in range(SEGS):
-        pooled(seg)[1]()
-        lax.fori_loop(seg * seg_rows, (seg + 1) * seg_rows, shift_halo, 0, unroll=True)
-        first = max(seg * per_seg - 1, 0)
-        last = (seg + 1) * per_seg - (0 if seg == SEGS - 1 else 1)
-        lax.fori_loop(first, last, second_conv, 0, unroll=True)
+                    plane = 48 * (2 * side + deep)
+                    own = fmap[plane : plane + 48, tile_at(i * 4 + row)]
+                    mpad[plane : plane + 48, tile_at(i * 4 + row + 1)] = (
+                        part + own.astype(F32)
+                    ).astype(BF16)
+        return 0
+
+    lax.fori_loop(0, hy // 2, second_conv, 0, unroll=4)
 
     def third_offset(product, b, at):
         return product[216 * b : 216 * b + 216, at]
@@ -562,12 +590,14 @@
             pltpu.VMEM((32, cells), BF16),
             pltpu.VMEM((240, cells + 2 * LANES), BF16),
             pltpu.VMEM((192, cells), BF16),
-            pltpu.VMEM((576, hcells + 2 * LANES), BF16),
+            pltpu.VMEM((96, hcells), BF16),
+            pltpu.VMEM((576, hcells // 2), BF16),
+            pltpu.VMEM((576, hcells // 2 + 2 * LANES), F32),
             pltpu.VMEM((192, cells + 2 * LANES), BF16),
             pltpu.VMEM((72, cells), F32),
             pltpu.VMEM((32, cells), BF16),
             pltpu.VMEM((32, cells), BF16),
-            pltpu.VMEM((192, 1728), BF16),
+            pltpu.VMEM((576, 576), BF16),
             pltpu.VMEM((648, 192), BF16),
             pltpu.VMEM((n * per, blocks * PART), BF16),
             pltpu.VMEM((blocks * PART, BY * LANES), BF16),

time: 33.5 us -> 33 us (0.985)
  Pallas kernels: 31.7 us -> 31.3 us
    pallas_call x1, Pallas kernels: 31.7 us -> 31.3 us  [on_device(): pl.pallas_call(functools.partial(kernel, n, ny), out_shape=jax.ShapeDtype...]
where the time goes in v6:
time: 33 us; the launch traced here: 32.9 us
  Pallas kernels  31.3 us (95%)
  local copies, waits for them, and re-layouts  1.6 us (5%)
    pallas_call x1, Pallas kernels, on_device(): pl.pallas_call(functools.partial(kernel, n, ny), out_shape=jax.ShapeDtype...  31.3 us
    unnamed x1, local copies, waits for them, and re-layouts  1.6 us

profile of v6, /device:TPU:0, one launch (start us, length us, event | category | flops | bytes accessed | tf_op | source)
XLA Modules:
  0.0 32.9 jit_solution(4433132420650298952)
XLA Ops:
  0.0 31.3 %shard_map.82 = bf16[16,2,1536]{2,1,0:T(2,128)(2,1)} custom-call(bf16[48,32,128]{2,1,0:T(8,128)(2,1)} %bitcast.3, bf16[48,324]{1,0:T(8,128)(2,1)} %w1_in.1, bf16[96,1296]{1,0:T(8,128)(2,1)} %w2_in.1, bf16[48,96]{1,0:T(8,128)(2,1)} %wl_in.1, bf16[12,1296]{1,0:T(8,128)(2,1)} %w3_in.1, bf16[3,12]{1,0:T(4,128)(2,1)} %wa_in.1, s32[1,32]{1,0:T(1,128)} %tissue_in.1, ...), custom_call_target="tpu_custom_call" | custom-call | flops 1600000000 | bytes 2000000 | tf_op jit(solution)/shard_map/pallas_call | solution.py:576
  31.3 1.6 %copy.10 = bf16[1,16,2,1536]{3,2,1,0:T(2,128)(2,1)} copy(bf16[1,16,2,1536]{3,2,1,0:T(2,128)(2,1)} %bitcast.2) | data formatting | bytes 196608

commit v7 on v6

--- a/solution.py
+++ b/solution.py
@@ -25,9 +25,9 @@
 
 def kernel(
     n, ny,
-    f_in, w1_in, w2_in, wl_in, w3_in, wa_in, tissue_in, owners_in,
+    f_ref, w1_ref, w2_ref, wl_ref, w3_ref, wa_ref, tissue_ref, owners_ref,
     out_ref,
-    f_ref, w1_ref, w2_ref, wl_ref, w3_ref, wa_ref, tissue_ref, owners_ref, own_sem, planes,
+    planes,
     rim_ref, w1_band, carry, carry3, landing, fhalo, xpad, fmap, rows_max, pool, shares, mpad, terms, edge, ehalo, w2_band, w3_band, picks, masked, tiles, outgoing,
     fsend, frecv, psend, precv, esend, erecv, asend, arecv,
 ):
@@ -40,15 +40,6 @@
     hy = ny // 2
     hcells = hy * LANES
 
-    sources = (f_in, w1_in, w2_in, wl_in, w3_in, wa_in, tissue_in, owners_in)
-    held_here = (f_ref, w1_ref, w2_ref, wl_ref, w3_ref, wa_ref, tissue_ref, owners_ref)
-    loads = [
-        pltpu.make_async_copy(source, place, own_sem.at[k])
-        for k, (source, place) in enumerate(zip(sources, held_here))
-    ]
-    for load in loads:
-        load.start()
-
     barrier = pltpu.get_barrier_semaphore()
 
     def greet(step, _):
@@ -121,7 +112,6 @@
     depth = 4
     f_rows = f_ref.shape[0]
     channels_in = f_rows // depth
-    loads[0].wait()
     planes[...] = f_ref[...].reshape(f_rows * ny, LANES).astype(F32)
     rim_pad = jnp.zeros((16 - channels_in, LANES), F32)
     for y in range(ny):
@@ -138,9 +128,6 @@
         rim_ref.at[0:16], fhalo.at[16:32], rim_ref.at[16:32], fhalo.at[0:16], fsend, frecv, 0
     )
     features_start()
-    for load in loads[1:]:
-        load.wait()
-
     nbx = LANES // BX
     count = tissue_ref.shape[1]
     blocks = (ny // BY) * nbx
@@ -576,11 +563,9 @@
     routed = pl.pallas_call(
         functools.partial(kernel, n, ny),
         out_shape=jax.ShapeDtypeStruct((n, SEND_CAP, w_affine.shape[0] * depth * LANES), BF16),
-        in_specs=[pl.BlockSpec(memory_space=pltpu.HBM)] * len(operands),
+        in_specs=[vmem] * len(operands),
         out_specs=vmem,
         scratch_shapes=[
-            *[pltpu.VMEM(operand.shape, operand.dtype) for operand in operands],
-            pltpu.SemaphoreType.DMA((len(operands),)),
             pltpu.VMEM((channels * depth * ny, LANES), F32),
             pltpu.VMEM((32, cells), BF16),
             pltpu.VMEM((576, 240), BF16),
@@ -613,7 +598,7 @@
             pltpu.SemaphoreType.DMA((2, n)),
         ],
         compiler_params=pltpu.CompilerParams(
-            collective_id=0, has_side_effects=True, vmem_limit_bytes=63 * 1024 * 1024
+            collective_id=0, has_side_effects=True, vmem_limit_bytes=48 * 1024 * 1024
         ),
         cost_estimate=pl.CostEstimate(
             flops=1600000000, bytes_accessed=2000000, transcendentals=65536

time: 33 us -> 37.1 us (1.12)
  local copies, waits for them, and re-layouts: 1.6 us -> 6.2 us
  Pallas kernels: 31.3 us -> 30.5 us
    unnamed x1 -> x17, local copies, waits for them, and re-layouts: 1.6 us -> 6.2 us
    pallas_call x1, Pallas kernels: 31.3 us -> 30.5 us  [on_device(): pl.pallas_call(functools.partial(kernel, n, ny), out_shape=jax.ShapeDtype...]
where the time goes in v7:
time: 37.1 us; the launch traced here: 36.7 us
  Pallas kernels  30.5 us (82%)
  local copies, waits for them, and re-layouts  6.2 us (17%)
    pallas_call x1, Pallas kernels, on_device(): pl.pallas_call(functools.partial(kernel, n, ny), out_shape=jax.ShapeDtype...  30.5 us
    unnamed x17, local copies, waits for them, and re-layouts  6.2 us

profile of v7, /device:TPU:0, one launch (start us, length us, event | category | flops | bytes accessed | tf_op | source)
XLA Modules:
  0.0 36.7 jit_solution(15880340542642406742)
XLA Ops:
  0.0 0.0 copy-start.6
  0.0 0.0 copy-start.5
  0.0 0.7 %copy-done.6 = s32[1,32]{1,0:T(1,128)S(1)} copy-done((s32[1,32]{1,0:T(1,128)S(1)}, s32[1,32]{1,0:T(1,128)}, u32[]{:S(2)}) %copy-start.6) | copy-done | bytes 152
  0.7 0.0 copy-done.5
  0.7 0.0 copy-start
  0.7 1.0 %copy-done = bf16[12,4,32,128]{3,2,1,0:T(8,128)(2,1)S(1)} copy-done((bf16[12,4,32,128]{3,2,1,0:T(8,128)(2,1)S(1)}, bf16[12,4,32,128]{3,2,1,0:T(8,128)(2,1)}, u32[]{:S(2)}) %copy-start) | copy-done | bytes 393240
  1.7 0.0 copy-start.1
  1.7 1.0 %copy-done.1 = bf16[96,1296]{1,0:T(8,128)(2,1)S(1)} copy-done((bf16[96,1296]{1,0:T(8,128)(2,1)S(1)}, bf16[96,1296]{1,0:T(8,128)(2,1)}, u32[]{:S(2)}) %copy-start.1) | copy-done | bytes 248856
  2.6 0.0 copy-start.2
  2.6 0.8 %copy-done.2 = bf16[12,1296]{1,0:T(8,128)(2,1)S(1)} copy-done((bf16[12,1296]{1,0:T(8,128)(2,1)S(1)}, bf16[12,1296]{1,0:T(8,128)(2,1)}, u32[]{:S(2)}) %copy-start.2) | copy-done | bytes 31128
  3.4 0.0 copy-start.3
  3.4 0.8 %copy-done.3 = bf16[48,324]{1,0:T(8,128)(2,1)S(1)} copy-done((bf16[48,324]{1,0:T(8,128)(2,1)S(1)}, bf16[48,324]{1,0:T(8,128)(2,1)}, u32[]{:S(2)}) %copy-start.3) | copy-done | bytes 31128
  4.2 0.0 copy-start.4
  4.2 0.7 %copy-done.4 = bf16[48,96]{1,0:T(8,128)(2,1)S(1)} copy-done((bf16[48,96]{1,0:T(8,128)(2,1)S(1)}, bf16[48,96]{1,0:T(8,128)(2,1)}, u32[]{:S(2)}) %copy-start.4) | copy-done | bytes 9240
  4.9 0.0 copy-start.7
  4.9 0.7 %copy-done.7 = s32[1,32]{1,0:T(1,128)S(1)} copy-done((s32[1,32]{1,0:T(1,128)S(1)}, s32[1,32]{1,0:T(1,128)}, u32[]{:S(2)}) %copy-start.7) | copy-done | bytes 152
  5.6 30.5 %shard_map.82 = bf16[16,2,1536]{2,1,0:T(2,128)(2,1)S(1)} custom-call(bf16[48,32,128]{2,1,0:T(8,128)(2,1)S(1)} %bitcast.3, bf16[48,324]{1,0:T(8,128)(2,1)S(1)} %copy-done.3, bf16[96,1296]{1,0:T(8,128)(2,1)S(1)} %copy-done.1, bf16[48,96]{1,0:T(8,128)(2,1)S(1)} %copy-done.4, bf16[12,1296]{1,0:T(8,128)(2,1)S(1)} %copy-done.2, bf16[3,12]{1,0:T(4,128)(2,1)S(1)} %copy-done.5, ...), custom_call_target="tpu_custom_call" | custom-call | flops 1600000000 | bytes 2000000 | tf_op jit(solution)/shard_map/pallas_call | solution.py:563
  36.1 0.6 %copy.10 = bf16[1,16,2,1536]{3,2,1,0:T(2,128)(2,1)} copy(bf16[1,16,2,1536]{3,2,1,0:T(2,128)(2,1)S(1)} %bitcast.2) | data formatting | bytes 196608
Async XLA Ops:
  0.0 0.7 %copy-start.6 = (s32[1,32]{1,0:T(1,128)S(1)}, s32[1,32]{1,0:T(1,128)}, u32[]{:S(2)}) copy-start(s32[1,32]{1,0:T(1,128)} %tissue_ref.1) | copy-start | bytes 388
  0.0 0.7 %copy-start.5 = (bf16[3,12]{1,0:T(4,128)(2,1)S(1)}, bf16[3,12]{1,0:T(4,128)(2,1)}, u32[]{:S(2)}) copy-start(bf16[3,12]{1,0:T(4,128)(2,1)} %wa_ref.1) | copy-start | bytes 220
  0.7 1.0 %copy-start = (bf16[12,4,32,128]{3,2,1,0:T(8,128)(2,1)S(1)}, bf16[12,4,32,128]{3,2,1,0:T(8,128)(2,1)}, u32[]{:S(2)}) copy-start(bf16[12,4,32,128]{3,2,1,0:T(8,128)(2,1)} %param.8) | copy-start | bytes 1179652
  1.7 1.0 %copy-start.1 = (bf16[96,1296]{1,0:T(8,128)(2,1)S(1)}, bf16[96,1296]{1,0:T(8,128)(2,1)}, u32[]{:S(2)}) copy-start(bf16[96,1296]{1,0:T(8,128)(2,1)} %w2_ref.1) | copy-start | bytes 746500
  2.6 0.8 %copy-start.2 = (bf16[12,1296]{1,0:T(8,128)(2,1)S(1)}, bf16[12,1296]{1,0:T(8,128)(2,1)}, u32[]{:S(2)}) copy-start(bf16[12,1296]{1,0:T(8,128)(2,1)} %w3_ref.1) | copy-start | bytes 93316
  3.4 0.8 %copy-start.3 = (bf16[48,324]{1,0:T(8,128)(2,1)S(1)}, bf16[48,324]{1,0:T(8,128)(2,1)}, u32[]{:S(2)}) copy-start(bf16[48,324]{1,0:T(8,128)(2,1)} %w1_ref.1) | copy-start | bytes 93316
  4.2 0.7 %copy-start.4 = (bf16[48,96]{1,0:T(8,128)(2,1)S(1)}, bf16[48,96]{1,0:T(8,128)(2,1)}, u32[]{:S(2)}) copy-start(bf16[48,96]{1,0:T(8,128)(2,1)} %wl_ref.1) | copy-start | bytes 27652
  4.9 0.7 %copy-start.7 = (s32[1,32]{1,0:T(1,128)S(1)}, s32[1,32]{1,0:T(1,128)}, u32[]{:S(2)}) copy-start(s32[1,32]{1,0:T(1,128)} %owners_ref.1) | copy-start | bytes 388
